TPU v7x, 128 devices: a whole 4x4x4 slice. The times are simulated.
128 devices in a mesh: leaf: 128 (over y, x, z, core).
Axes of the slice: x: 4, y: 4, z: 4, core: 2. Of those that a mesh axis runs over, the one named last changes fastest.
Arguments:
- leaf_bases: float32 [4096, 64, 256], P('leaf'), may hold values from -0.4 to 0.4
- transfers: float32 [8064, 64, 64], P('leaf')
- top_transfers: float32 [126, 64, 64], replicated
- couplings: float32 [7168, 8, 64, 64], P('leaf'), may hold values from -6 to 6
- coupling_cols: int32 [7168, 8], P('leaf'), may hold values from 0 to 7167, as said below
Outputs:
- new_leaf_bases: float32 [4096, 64, 256], P('leaf')
- new_transfers: float32 [8064, 64, 64], P('leaf')
- new_top: float32 [126, 64, 64], replicated
- root_factor: float32 [64, 64], replicated
- new_couplings: float32 [7168, 8, 64, 64], P('leaf')
Inputs may be any that keep to these rules, and one draw needn't show every extreme that they name: `coupling_cols`: each entry names a cluster of the same tree level as its row's cluster, never that cluster itself, stored on a device at most 8 away from the row's device; the first two entries of every row lie exactly 8 devices away.
All inputs are finite; a program needn't handle non-finite values.
Results may differ from a plain program's by a relative error of at most 0.0001.
Values sent between devices are 32-bit elements; how exact they have to be, the bound alone decides.
No kernel may reach another device: no remote copies, remote signals or barrier semaphores. Data moves between devices by JAX's collectives and lax.ppermute only.
A program may use at most 256 MiB of HBM per device.

v0:
```python
import jax
import jax.numpy as jnp
from jax import lax
from jax.sharding import PartitionSpec as P

HOP = 8


PRECISE = lax.Precision.HIGHEST


def shifted(array, axis, by):
    devices = lax.axis_size(axis)
    pairs = [(i, i + by) for i in range(devices) if 0 <= i + by < devices]
    return lax.ppermute(array, axis, pairs)


def inverse_lower(factor):
    identity = jnp.broadcast_to(jnp.eye(factor.shape[-1], dtype=factor.dtype), factor.shape)
    return lax.linalg.triangular_solve(factor, identity, left_side=True, lower=True)


def join_pairs(lower_part, upper_part):
    gram_matrix = jnp.einsum("bki,bkj->bij", lower_part, lower_part, precision=PRECISE)
    gram_matrix = gram_matrix + jnp.einsum(
        "bki,bkj->bij", upper_part, upper_part, precision=PRECISE
    )
    factor = jnp.linalg.cholesky(gram_matrix)
    inverse = inverse_lower(factor)
    stacked = jnp.concatenate([lower_part, upper_part], axis=1)
    solved = jnp.einsum("bki,bji->bkj", stacked, inverse, precision=PRECISE)
    rank_size = lower_part.shape[1]
    return (factor, solved[:, 0:rank_size], solved[:, rank_size:])


def carry_up(factor, transfer):
    return jnp.einsum("bki,bkj->bij", factor, transfer, precision=PRECISE)


def pair_order(lower_q, upper_q):
    return jnp.stack([lower_q, upper_q], axis=1).reshape((-1,) + lower_q.shape[1:])


def on_device(leaf_bases, transfers, top_transfers, couplings, coupling_cols):
    leaf_dev = leaf_bases.shape[0]
    tree_depth = leaf_dev.bit_length() - 1
    devices = lax.axis_size("leaf")
    top_depth = devices.bit_length() - 1
    own_index = lax.axis_index("leaf")
    gram_matrix = jnp.einsum("bip,bjp->bij", leaf_bases, leaf_bases, precision=PRECISE)
    factor = jnp.linalg.cholesky(gram_matrix)
    new_leaves = jnp.einsum("bij,bjp->bip", inverse_lower(factor), leaf_bases, precision=PRECISE)
    factors = [factor]
    new_local = []
    offset = 0
    carried = carry_up(factor, transfers[0:leaf_dev])
    for height in range(1, tree_depth + 1):
        offset = offset + (leaf_dev >> height - 1)
        factor, lower_q, upper_q = join_pairs(carried[0::2], carried[1::2])
        new_local.append(pair_order(lower_q, upper_q))
        factors.append(factor)
        carried = carry_up(factor, transfers[offset : offset + (leaf_dev >> height)])
    frontier = lax.all_gather(carried, "leaf", axis=0, tiled=True)
    upper_new = []
    for section_bit in range(top_depth):
        factor, lower_q, upper_q = join_pairs(frontier[0::2], frontier[1::2])
        joined = pair_order(lower_q, upper_q)
        if section_bit == 0:
            own_root = lax.dynamic_slice_in_dim(joined, own_index, 1, 0)
        else:
            upper_new.append(joined)
        if section_bit < top_depth - 1:
            first_node = 2 ** (top_depth - section_bit - 1) - 2
            frontier = carry_up(factor, top_transfers[first_node : first_node + factor.shape[0]])
    root_low = factor[0]
    new_transfers = jnp.concatenate(new_local + [own_root], axis=0)
    new_top = jnp.concatenate(upper_new[::-1], axis=0)
    root_factor = root_low.T
    packed = jnp.concatenate(factors[0:3], axis=0)
    row_dev = packed.shape[0]
    pieces = []
    for reach_dev in range(-HOP, HOP + 1):
        if reach_dev == 0:
            pieces.append(packed)
        else:
            pieces.append(shifted(packed, "leaf", -reach_dev))
    window = jnp.concatenate(pieces, axis=0)
    device_of = coupling_cols // row_dev
    slot_index = (device_of - own_index + HOP) * row_dev + coupling_cols % row_dev
    column_factor = jnp.take(window, slot_index.reshape(-1), axis=0).reshape(
        coupling_cols.shape + window.shape[1:]
    )
    left_side = jnp.einsum("rki,rckl->rcil", packed, couplings, precision=PRECISE)
    new_couplings = jnp.einsum("rcil,rclj->rcij", left_side, column_factor, precision=PRECISE)
    return (new_leaves, new_transfers, new_top, root_factor, new_couplings)


def solution(mesh):
    in_specs = (
        P("leaf", None, None),
        P("leaf", None, None),
        P(),
        P("leaf", None, None, None),
        P("leaf", None),
    )
    out_specs = (
        P("leaf", None, None),
        P("leaf", None, None),
        P(),
        P(),
        P("leaf", None, None, None),
    )
    return jax.shard_map(
        on_device, mesh=mesh, in_specs=in_specs, out_specs=out_specs, check_vma=False
    )
```

profile of v0, /device:TPU:7, one launch (start us, length us, event | category | flops | bytes accessed | tf_op | source)
XLA Modules:
  0.0 2403.1 jit_solution(1317359433780959746)
XLA Ops:
  14.5 188.7 %custom-call.57 = f32[32,64,64]{2,1,0:T(8,128)S(1)} custom-call(f32[32,64,64]{2,1,0:T(8,128)} %fusion.15), custom_call_target="Cholesky" | custom-call | tf_op jit(solution)/shard_map/jit(cholesky)/cholesky | solution.py:51
  222.7 95.2 %custom-call.59 = f32[16,64,64]{2,1,0:T(8,128)} custom-call(f32[16,64,64]{2,1,0:T(8,128)} %fusion.33), custom_call_target="Cholesky" | custom-call | tf_op jit(solution)/shard_map/jit(cholesky)/cholesky | solution.py:28
  333.5 47.8 %custom-call.61 = f32[8,64,64]{2,1,0:T(8,128)S(1)} custom-call(f32[8,64,64]{2,1,0:T(8,128)} %fusion.54), custom_call_target="Cholesky" | custom-call | tf_op jit(solution)/shard_map/jit(cholesky)/cholesky | solution.py:28
  385.8 5.3 pad_maximum_fusion.2
  391.1 3.6 copy.426
  397.9 4.0 collective-permute-start.1
  401.8 5.7 collective-permute-start.2
  409.7 5.2 collective-permute-start.4
  421.5 24.8 %custom-call.63 = f32[4,64,64]{2,1,0:T(8,128)} custom-call(f32[4,64,64]{2,1,0:T(8,128)} %fusion.77), custom_call_target="Cholesky" | custom-call | tf_op jit(solution)/shard_map/jit(cholesky)/cholesky | solution.py:28
  451.8 12.5 custom-call.65
  467.3 6.6 custom-call.67
  477.0 5.4 fusion.271
  488.9 3.9 copy.499
  492.8 5.7 custom-call.68
  499.7 40.7 %custom-call.62 = f32[8,1,64,64]{2,3,1,0:T(8,128)} custom-call(f32[8,1,64,64]{3,2,1,0:T(8,128)} %get-tuple-element.43), custom_call_target="InvertDiagBlocksLowerTriangular" | custom-call | tf_op jit(solution)/shard_map/triangular_solve/custom-call.9 | solution.py:20
  544.3 80.0 %custom-call.60 = f32[16,1,64,64]{2,3,1,0:T(8,128)} custom-call(f32[16,1,64,64]{3,2,1,0:T(8,128)} %get-tuple-element.45), custom_call_target="InvertDiagBlocksLowerTriangular" | custom-call | tf_op jit(solution)/shard_map/triangular_solve/custom-call.8 | solution.py:20
  629.4 69.0 %custom-call.58 = f32[32,1,64,64]{0,2,3,1:T(8,128)} custom-call(f32[32,1,64,64]{0,3,2,1:T(8,128)} %get-tuple-element.47), custom_call_target="InvertDiagBlocksLowerTriangular" | custom-call | tf_op jit(solution)/shard_map/triangular_solve/custom-call.7 | solution.py:20
  698.4 3.9 copy.324
  707.8 19.6 fusion.238
  740.0 4.2 copy.507
  744.1 3.9 copy.508
  748.0 3.5 copy.509
  751.6 3.4 copy.510
  755.0 3.3 copy.511
  787.8 4.3 collective-permute-start.9
  795.1 19.7 collective-permute-done.5
  818.2 33.1 %collective-permute-done.6 = f32[56,64,64]{2,1,0:T(8,128)S(1)} collective-permute-done((f32[56,64,64]{2,1,0:T(8,128)S(1)}, f32[56,64,64]{2,1,0:T(8,128)S(1)}, u32[]{:S(2)}, u32[]{:S(2)}) %collective-permute-start.6) | collective-permute-done | bytes 917536 | tf_op jit(solution)/shard_map/ppermute | solution.py:15
  854.7 12.1 collective-permute-done.7
  866.8 6.2 collective-permute-start.12
  875.6 3.6 collective-permute-start.13
  880.7 25.5 %collective-permute-start.14 = (f32[56,64,64]{2,1,0:T(8,128)S(1)}, f32[56,64,64]{2,1,0:T(8,128)S(1)}, u32[]{:S(2)}, u32[]{:S(2)}) collective-permute-start(f32[56,64,64]{2,1,0:T(8,128)S(1)} %copy-done.23), channel_id=1, source_target_pairs={{7,0},{8,1},{9,2},{10,3},{11,4},{12,5},{13,6},{14,7},{15,8},{16,9}... | collective-permute-start | bytes 2752520 | tf_op jit(solution)/shard_map/ppermute | solution.py:15
  907.7 80.6 %collective-permute-done.10 = f32[56,64,64]{2,1,0:T(8,128)S(1)} collective-permute-done((f32[56,64,64]{2,1,0:T(8,128)S(1)}, f32[56,64,64]{2,1,0:T(8,128)S(1)}, u32[]{:S(2)}, u32[]{:S(2)}) %collective-permute-start.10) | collective-permute-done | bytes 917536 | tf_op jit(solution)/shard_map/ppermute | solution.py:15
  995.3 30.2 %collective-permute-done.12 = f32[56,64,64]{2,1,0:T(8,128)S(1)} collective-permute-done((f32[56,64,64]{2,1,0:T(8,128)S(1)}, f32[56,64,64]{2,1,0:T(8,128)S(1)}, u32[]{:S(2)}, u32[]{:S(2)}) %collective-permute-start.12) | collective-permute-done | bytes 917536 | tf_op jit(solution)/shard_map/ppermute | solution.py:15
  1027.0 37.8 %collective-permute-done.13 = f32[56,64,64]{2,1,0:T(8,128)S(1)} collective-permute-done((f32[56,64,64]{2,1,0:T(8,128)S(1)}, f32[56,64,64]{2,1,0:T(8,128)S(1)}, u32[]{:S(2)}, u32[]{:S(2)}) %collective-permute-start.13) | collective-permute-done | bytes 917536 | tf_op jit(solution)/shard_map/ppermute | solution.py:15
  1066.3 63.7 %collective-permute-done.14 = f32[56,64,64]{2,1,0:T(8,128)S(1)} collective-permute-done((f32[56,64,64]{2,1,0:T(8,128)S(1)}, f32[56,64,64]{2,1,0:T(8,128)S(1)}, u32[]{:S(2)}, u32[]{:S(2)}) %collective-permute-start.14) | collective-permute-done | bytes 917536 | tf_op jit(solution)/shard_map/ppermute | solution.py:15
  1131.4 12.0 collective-permute-done.15
  1144.9 17.0 gather_fusion
  1161.9 22.9 fusion
  1184.8 5.9 fusion.219
  1190.7 3.6 convolution_add_fusion
  1196.1 3.5 fusion.9
  1199.6 376.8 %custom-call.43 = f32[64,64,64]{2,1,0:T(8,128)} custom-call(f32[64,64,64]{2,1,0:T(8,128)} %fusion.9), custom_call_target="Cholesky" | custom-call | tf_op jit(solution)/shard_map/jit(cholesky)/cholesky | solution.py:28
  1582.4 4.0 copy.374
  1586.4 4.3 fusion.236
  1596.3 187.5 %custom-call.69 = f32[32,64,64]{2,1,0:T(8,128)S(1)} custom-call(f32[32,64,64]{2,1,0:T(8,128)S(1)} %fusion.14), custom_call_target="Cholesky" | custom-call | tf_op jit(solution)/shard_map/jit(cholesky)/cholesky | solution.py:28
  1795.1 94.2 %custom-call.70 = f32[16,64,64]{2,1,0:T(8,128)S(1)} custom-call(f32[16,64,64]{2,1,0:T(8,128)S(1)} %fusion.30), custom_call_target="Cholesky" | custom-call | tf_op jit(solution)/shard_map/jit(cholesky)/cholesky | solution.py:28
  1893.3 46.9 %custom-call.71 = f32[8,64,64]{2,1,0:T(8,128)S(1)} custom-call(f32[8,64,64]{2,1,0:T(8,128)S(1)} %fusion.51), custom_call_target="Cholesky" | custom-call | tf_op jit(solution)/shard_map/jit(cholesky)/cholesky | solution.py:28
  1943.2 23.5 custom-call.72
  1969.2 11.7 custom-call.73
  1983.6 4.9 fusion.222
  1988.4 67.4 %custom-call.80 = f32[32,1,64,64]{0,2,3,1:T(8,128)S(1)} custom-call(f32[32,1,64,64]{0,3,2,1:T(8,128)} %get-tuple-element.39), custom_call_target="InvertDiagBlocksLowerTriangular" | custom-call | tf_op jit(solution)/shard_map/triangular_solve/custom-call.7 | solution.py:20
  2064.2 80.0 %custom-call.79 = f32[16,1,64,64]{2,3,1,0:T(8,128)} custom-call(f32[16,1,64,64]{3,2,1,0:T(8,128)} %select_bitcast_fusion.3), custom_call_target="InvertDiagBlocksLowerTriangular" | custom-call | tf_op jit(solution)/shard_map/triangular_solve/custom-call.8 | solution.py:20
  2149.9 40.7 %custom-call.78 = f32[8,1,64,64]{2,3,1,0:T(8,128)} custom-call(f32[8,1,64,64]{3,2,1,0:T(8,128)} %select_bitcast_fusion.5), custom_call_target="InvertDiagBlocksLowerTriangular" | custom-call | tf_op jit(solution)/shard_map/triangular_solve/custom-call.9 | solution.py:20
  2196.6 21.0 custom-call.77
  2222.1 11.4 custom-call.76
  2239.3 5.8 custom-call.74
  2246.5 5.5 custom-call.75
  2263.0 4.8 copy.444
  2268.5 68.5 %custom-call.44 = f32[64,1,64,64]{0,2,3,1:T(8,128)} custom-call(f32[64,1,64,64]{0,3,2,1:T(8,128)} %get-tuple-element.41), custom_call_target="InvertDiagBlocksLowerTriangular" | custom-call | tf_op jit(solution)/shard_map/triangular_solve | solution.py:20
  2337.0 3.3 copy.369
  2342.5 8.2 fusion.5
  2353.9 5.7 copy.371
  2359.6 10.6 custom-call.66
  2371.0 20.5 custom-call.64
  (344 shorter events, 252.8 us)
Async XLA Ops:
  7.2 1.6 copy-start
  7.2 1177.6 %all-gather.3.cloned.1.call-start = ((), (), s32[]{:S(2)}) async-start(), calls=%async_computation | async-start | bytes 4227072 | tf_op jit(solution)/shard_map/all_gather | solution.py:63
  205.2 2.2 copy-start.3
  215.8 1.0 copy-start.5
  321.1 0.8 copy-start.7
  394.7 369.0 %collective-permute-start = (f32[56,64,64]{2,1,0:T(8,128)}, f32[56,64,64]{2,1,0:T(8,128)}, u32[]{:S(2)}, u32[]{:S(2)}) collective-permute-start(f32[56,64,64]{2,1,0:T(8,128)} %copy.426), channel_id=1, source_target_pairs={{0,8},{1,9},{2,10},{3,11},{4,12},{5,13},{6,14},{7,15},{8,16},{9,17... | collective-permute-start | bytes 2752520 | tf_op jit(solution)/shard_map/ppermute | solution.py:15
  397.9 370.2 %collective-permute-start.1 = (f32[56,64,64]{2,1,0:T(8,128)}, f32[56,64,64]{2,1,0:T(8,128)}, u32[]{:S(2)}, u32[]{:S(2)}) collective-permute-start(f32[56,64,64]{2,1,0:T(8,128)} %copy.426), channel_id=1, source_target_pairs={{0,7},{1,8},{2,9},{3,10},{4,11},{5,12},{6,13},{7,14},{8,15},{9,16}... | collective-permute-start | bytes 2752520 | tf_op jit(solution)/shard_map/ppermute | solution.py:15
  401.8 372.2 %collective-permute-start.2 = (f32[56,64,64]{2,1,0:T(8,128)}, f32[56,64,64]{2,1,0:T(8,128)}, u32[]{:S(2)}, u32[]{:S(2)}) collective-permute-start(f32[56,64,64]{2,1,0:T(8,128)} %copy.426), channel_id=1, source_target_pairs={{0,6},{1,7},{2,8},{3,9},{4,10},{5,11},{6,12},{7,13},{8,14},{9,15},... | collective-permute-start | bytes 2752520 | tf_op jit(solution)/shard_map/ppermute | solution.py:15
  407.5 375.0 %collective-permute-start.3 = (f32[56,64,64]{2,1,0:T(8,128)}, f32[56,64,64]{2,1,0:T(8,128)}, u32[]{:S(2)}, u32[]{:S(2)}) collective-permute-start(f32[56,64,64]{2,1,0:T(8,128)} %copy.426), channel_id=1, source_target_pairs={{0,5},{1,6},{2,7},{3,8},{4,9},{5,10},{6,11},{7,12},{8,13},{9,14},{... | collective-permute-start | bytes 2752520 | tf_op jit(solution)/shard_map/ppermute | solution.py:15
  409.7 378.1 %collective-permute-start.4 = (f32[56,64,64]{2,1,0:T(8,128)}, f32[56,64,64]{2,1,0:T(8,128)}, u32[]{:S(2)}, u32[]{:S(2)}) collective-permute-start(f32[56,64,64]{2,1,0:T(8,128)} %copy.426), channel_id=1, source_target_pairs={{0,4},{1,5},{2,6},{3,7},{4,8},{5,9},{6,10},{7,11},{8,12},{9,13},{1... | collective-permute-start | bytes 2752520 | tf_op jit(solution)/shard_map/ppermute | solution.py:15
  447.3 18.9 copy-start.46
  465.0 1.2 copy-start.49
  476.9 7.4 copy-start.25
  476.9 8.0 copy-start.12
  482.3 3.5 copy-start.6
  486.9 11.8 copy-start.44
  704.6 3.2 copy-start.11
  707.8 19.7 copy-start.45
  707.8 19.7 copy-start.21
  707.8 19.7 copy-start.22
  707.8 20.8 copy-start.30
  707.8 20.8 copy-start.31
  727.5 2.0 copy-start.17
  727.5 2.7 copy-start.43
  727.5 2.7 copy-start.2
  737.9 2.0 copy-start.48
  763.6 1.5 copy-start.23
  765.1 49.7 %collective-permute-start.5 = (f32[56,64,64]{2,1,0:T(8,128)S(1)}, f32[56,64,64]{2,1,0:T(8,128)S(1)}, u32[]{:S(2)}, u32[]{:S(2)}) collective-permute-start(f32[56,64,64]{2,1,0:T(8,128)S(1)} %copy-done.23), channel_id=1, source_target_pairs={{0,3},{1,4},{2,5},{3,6},{4,7},{5,8},{6,9},{7,10},{8,11},{9,12},{10... | collective-permute-start | bytes 2752520 | tf_op jit(solution)/shard_map/ppermute | solution.py:15
  768.1 5.9 copy-start.34
  768.1 83.2 %collective-permute-start.6 = (f32[56,64,64]{2,1,0:T(8,128)S(1)}, f32[56,64,64]{2,1,0:T(8,128)S(1)}, u32[]{:S(2)}, u32[]{:S(2)}) collective-permute-start(f32[56,64,64]{2,1,0:T(8,128)S(1)} %copy-done.23), channel_id=1, source_target_pairs={{0,2},{1,3},{2,4},{3,5},{4,6},{5,7},{6,8},{7,9},{8,10},{9,11},{10,... | collective-permute-start | bytes 2752520 | tf_op jit(solution)/shard_map/ppermute | solution.py:15
  774.0 92.8 %collective-permute-start.7 = (f32[56,64,64]{2,1,0:T(8,128)S(1)}, f32[56,64,64]{2,1,0:T(8,128)S(1)}, u32[]{:S(2)}, u32[]{:S(2)}) collective-permute-start(f32[56,64,64]{2,1,0:T(8,128)S(1)} %copy-done.23), channel_id=1, source_target_pairs={{0,1},{1,2},{2,3},{3,4},{4,5},{5,6},{6,7},{7,8},{8,9},{9,10},{10,1... | collective-permute-start | bytes 2752520 | tf_op jit(solution)/shard_map/ppermute | solution.py:15
  782.5 93.0 %collective-permute-start.8 = (f32[56,64,64]{2,1,0:T(8,128)S(1)}, f32[56,64,64]{2,1,0:T(8,128)S(1)}, u32[]{:S(2)}, u32[]{:S(2)}) collective-permute-start(f32[56,64,64]{2,1,0:T(8,128)S(1)} %copy-done.23), channel_id=1, source_target_pairs={{1,0},{2,1},{3,2},{4,3},{5,4},{6,5},{7,6},{8,7},{9,8},{10,9},{11,1... | collective-permute-start | bytes 2752520 | tf_op jit(solution)/shard_map/ppermute | solution.py:15
  787.8 92.9 %collective-permute-start.9 = (f32[56,64,64]{2,1,0:T(8,128)S(1)}, f32[56,64,64]{2,1,0:T(8,128)S(1)}, u32[]{:S(2)}, u32[]{:S(2)}) collective-permute-start(f32[56,64,64]{2,1,0:T(8,128)S(1)} %copy-done.23), channel_id=1, source_target_pairs={{2,0},{3,1},{4,2},{5,3},{6,4},{7,5},{8,6},{9,7},{10,8},{11,9},{12,... | collective-permute-start | bytes 2752520 | tf_op jit(solution)/shard_map/ppermute | solution.py:15
  814.8 173.4 %collective-permute-start.10 = (f32[56,64,64]{2,1,0:T(8,128)S(1)}, f32[56,64,64]{2,1,0:T(8,128)S(1)}, u32[]{:S(2)}, u32[]{:S(2)}) collective-permute-start(f32[56,64,64]{2,1,0:T(8,128)S(1)} %copy-done.23), channel_id=1, source_target_pairs={{3,0},{4,1},{5,2},{6,3},{7,4},{8,5},{9,6},{10,7},{11,8},{12,9},{13... | collective-permute-start | bytes 2752520 | tf_op jit(solution)/shard_map/ppermute | solution.py:15
  851.3 142.5 %collective-permute-start.11 = (f32[56,64,64]{2,1,0:T(8,128)S(1)}, f32[56,64,64]{2,1,0:T(8,128)S(1)}, u32[]{:S(2)}, u32[]{:S(2)}) collective-permute-start(f32[56,64,64]{2,1,0:T(8,128)S(1)} %copy-done.23), channel_id=1, source_target_pairs={{4,0},{5,1},{6,2},{7,3},{8,4},{9,5},{10,6},{11,7},{12,8},{13,9},{1... | collective-permute-start | bytes 2752520 | tf_op jit(solution)/shard_map/ppermute | solution.py:15
  854.7 24.4 %copy-start.8 = (f32[16,64,64]{2,1,0:T(8,128)S(1)}, f32[16,64,64]{2,1,0:T(8,128)}, u32[]{:S(2)}) copy-start(f32[16,64,64]{2,1,0:T(8,128)} %copy-done.7) | copy-start | bytes 786436
  866.8 158.6 %collective-permute-start.12 = (f32[56,64,64]{2,1,0:T(8,128)S(1)}, f32[56,64,64]{2,1,0:T(8,128)S(1)}, u32[]{:S(2)}, u32[]{:S(2)}) collective-permute-start(f32[56,64,64]{2,1,0:T(8,128)S(1)} %copy-done.23), channel_id=1, source_target_pairs={{5,0},{6,1},{7,2},{8,3},{9,4},{10,5},{11,6},{12,7},{13,8},{14,9},{... | collective-permute-start | bytes 2752520 | tf_op jit(solution)/shard_map/ppermute | solution.py:15
  875.6 189.2 %collective-permute-start.13 = (f32[56,64,64]{2,1,0:T(8,128)S(1)}, f32[56,64,64]{2,1,0:T(8,128)S(1)}, u32[]{:S(2)}, u32[]{:S(2)}) collective-permute-start(f32[56,64,64]{2,1,0:T(8,128)S(1)} %copy-done.23), channel_id=1, source_target_pairs={{6,0},{7,1},{8,2},{9,3},{10,4},{11,5},{12,6},{13,7},{14,8},{15,9},... | collective-permute-start | bytes 2752520 | tf_op jit(solution)/shard_map/ppermute | solution.py:15
  880.7 249.2 %collective-permute-start.14 = (f32[56,64,64]{2,1,0:T(8,128)S(1)}, f32[56,64,64]{2,1,0:T(8,128)S(1)}, u32[]{:S(2)}, u32[]{:S(2)}) collective-permute-start(f32[56,64,64]{2,1,0:T(8,128)S(1)} %copy-done.23), channel_id=1, source_target_pairs={{7,0},{8,1},{9,2},{10,3},{11,4},{12,5},{13,6},{14,7},{15,8},{16,9}... | collective-permute-start | bytes 2752520 | tf_op jit(solution)/shard_map/ppermute | solution.py:15
  988.2 155.2 %collective-permute-start.15 = (f32[56,64,64]{2,1,0:T(8,128)S(1)}, f32[56,64,64]{2,1,0:T(8,128)S(1)}, u32[]{:S(2)}, u32[]{:S(2)}) collective-permute-start(f32[56,64,64]{2,1,0:T(8,128)S(1)} %copy-done.23), channel_id=1, source_target_pairs={{8,0},{9,1},{10,2},{11,3},{12,4},{13,5},{14,6},{15,7},{16,8},{17,9... | collective-permute-start | bytes 2752520 | tf_op jit(solution)/shard_map/ppermute | solution.py:15
  1184.8 5.9 copy-start.4
  1788.1 2.6 copy-start.13
  1794.8 95.6 %copy-start.18 = (f32[16,64,64]{1,2,0:T(8,128)S(1)}, f32[16,64,64]{1,2,0:T(8,128)}, u32[]{:S(2)}) copy-start(f32[16,64,64]{1,2,0:T(8,128)} %copy.509) | copy-start | bytes 786436
  1891.7 49.5 %copy-start.27 = (f32[8,64,64]{1,2,0:T(8,128)S(1)}, f32[8,64,64]{1,2,0:T(8,128)}, u32[]{:S(2)}) copy-start(f32[8,64,64]{1,2,0:T(8,128)} %copy.510) | copy-start | bytes 393220
  1893.2 73.6 %copy-start.26 = (f32[4,64,64]{2,1,0:T(8,128)S(1)}, f32[4,64,64]{2,1,0:T(8,128)}, u32[]{:S(2)}) copy-start(f32[4,64,64]{2,1,0:T(8,128)} %custom-call.63) | copy-start | bytes 196612
  1893.3 73.6 %copy-start.47 = (pred[4]{0:T(512)(128)(4,1)S(1)}, pred[4]{0:T(512)(128)(4,1)}, u32[]{:S(2)}) copy-start(pred[4]{0:T(512)(128)(4,1)} %copy-done.46) | copy-start | bytes 16
  1893.3 74.3 %copy-start.35 = (f32[4,64,64]{1,2,0:T(8,128)S(1)}, f32[4,64,64]{1,2,0:T(8,128)}, u32[]{:S(2)}) copy-start(f32[4,64,64]{1,2,0:T(8,128)} %copy.511) | copy-start | bytes 196612
  1941.6 39.5 %copy-start.33 = (f32[2,64,64]{2,1,0:T(8,128)S(1)}, f32[2,64,64]{2,1,0:T(8,128)}, u32[]{:S(2)}) copy-start(f32[2,64,64]{2,1,0:T(8,128)} %copy-done.32) | copy-start | bytes 98308
  1941.6 39.5 %copy-start.50 = (pred[2]{0:T(512)(128)(4,1)S(1)}, pred[2]{0:T(512)(128)(4,1)}, u32[]{:S(2)}) copy-start(pred[2]{0:T(512)(128)(4,1)} %copy-done.49) | copy-start | bytes 10
  1941.7 40.2 %copy-start.39 = (f32[2,64,64]{1,2,0:T(8,128)S(1)}, f32[2,64,64]{1,2,0:T(8,128)}, u32[]{:S(2)}) copy-start(f32[2,64,64]{1,2,0:T(8,128)} %copy.512) | copy-start | bytes 98308
  2057.4 1.2 copy-start.14
  2057.4 1.5 copy-start.15
  2062.2 84.1 %copy-start.19 = (f32[16,64,64]{1,2,0:T(8,128)S(1)}, f32[16,64,64]{1,2,0:T(8,128)}, u32[]{:S(2)}) copy-start(f32[16,64,64]{1,2,0:T(8,128)} %get-tuple-element.57) | copy-start | bytes 786436
  2062.2 84.1 %copy-start.20 = (f32[16,64,64]{1,2,0:T(8,128)S(1)}, f32[16,64,64]{1,2,0:T(8,128)}, u32[]{:S(2)}) copy-start(f32[16,64,64]{1,2,0:T(8,128)} %get-tuple-element.58) | copy-start | bytes 786436
  2147.3 44.9 %copy-start.29 = (f32[8,64,64]{1,2,0:T(8,128)S(1)}, f32[8,64,64]{1,2,0:T(8,128)}, u32[]{:S(2)}) copy-start(f32[8,64,64]{1,2,0:T(8,128)} %get-tuple-element.63) | copy-start | bytes 393220
  2193.6 25.4 %copy-start.38 = (f32[4,64,64]{1,2,0:T(8,128)S(1)}, f32[4,64,64]{1,2,0:T(8,128)}, u32[]{:S(2)}) copy-start(f32[4,64,64]{1,2,0:T(8,128)} %get-tuple-element.71) | copy-start | bytes 196612
  2340.3 2.0 copy-start.9
  2340.3 2.2 copy-start.10
  2353.9 16.6 copy-start.41
  2353.9 16.6 copy-start.42
  2353.9 38.0 %copy-start.36 = (f32[4,64,64]{1,2,0:T(8,128)S(1)}, f32[4,64,64]{1,2,0:T(8,128)}, u32[]{:S(2)}) copy-start(f32[4,64,64]{1,2,0:T(8,128)} %get-tuple-element.73) | copy-start | bytes 196612
  2353.9 38.0 %copy-start.37 = (f32[4,64,64]{1,2,0:T(8,128)S(1)}, f32[4,64,64]{1,2,0:T(8,128)}, u32[]{:S(2)}) copy-start(f32[4,64,64]{1,2,0:T(8,128)} %get-tuple-element.74) | copy-start | bytes 196612
  2370.5 23.5 copy-start.40
  2370.5 25.5 %copy-start.1 = (f32[32,64,256]{2,1,0:T(8,128)S(1)}, f32[32,64,256]{2,1,0:T(8,128)}, u32[]{:S(2)}) copy-start(f32[32,64,256]{2,1,0:T(8,128)} %param.23) | copy-start | bytes 6291460
  (4 other events, 2.7 us)
Sparse Core Ops, SparseCore 0:
  477.0 162.7 all-gather.2
where the time goes:
time: 2440 us; the launch traced here: 2400 us
  other arithmetic  1700 us (70%)
  waiting for transfers between devices  289 us (12%)
  local copies, waits for them, and re-layouts  187 us (8%)
  matrix products  130 us (5%)
  starting transfers between devices  76.9 us (3%)
    another operation x36, other arithmetic, join_pairs(): factor = jnp.linalg.cholesky(gram_matrix)  939 us
    another operation x24, other arithmetic, inverse_lower(): lax.linalg.triangular_solve(factor, identity, left_side=True, lower=True)  538 us
    ppermute x16, waiting for transfers between devices, shifted(): return lax.ppermute(array, axis, pairs)  289 us
    another operation x4, other arithmetic, on_device(): factor = jnp.linalg.cholesky(gram_matrix)  191 us
    ppermute x16, starting transfers between devices, shifted(): return lax.ppermute(array, axis, pairs)  76.8 us
    unnamed x138, local copies, waits for them, and re-layouts  73.5 us
  transfers between devices with their start and end apart: 17, of which 8 were waited for; matrix products, arithmetic and copies ran while one was open for 18% of the time, Pallas kernels for 0%

commit v1 on v0

v1 whole, which is shorter than its diff:
```python
import functools

import jax
import jax.numpy as jnp
from jax import lax
from jax.experimental import pallas as pl
from jax.experimental.pallas import tpu as pltpu
from jax.sharding import PartitionSpec as P

RANK = 64
LEAF = 32
NODES = 63
ROW = 56
CPL = 8
QUART = 14
UNIT = QUART + 1
COLUMN = 8
TOPN = 127
VMEM_LIMIT = 48 * 1024 * 1024
F32 = jnp.float32
BF16 = jnp.bfloat16
FULL = lax.Precision.HIGHEST

NN = (((1,), (0,)), ((), ()))
NT = (((1,), (1,)), ((), ()))
TN = (((0,), (0,)), ((), ()))


def exact(a, b, dims):
    return lax.dot_general(a, b, dims, precision=FULL, preferred_element_type=F32)


def split(a):
    high = a.astype(BF16)
    return high, (a - high.astype(F32)).astype(BF16)


def three(a, b, dims):
    ah, al = a
    bh, bl = b
    dot = functools.partial(lax.dot_general, dimension_numbers=dims, preferred_element_type=F32)
    return dot(ah, bh) + (dot(ah, bl) + dot(al, bh))


def mul3(a, b, dims):
    return three(split(a), split(b), dims)


def params():
    return pltpu.CompilerParams(vmem_limit_bytes=VMEM_LIMIT)


def load_lanes(g_ref, w_ref):
    place = lax.broadcasted_iota(jnp.int32, (RANK, 128), 0)

    def body(i, carry):
        block = g_ref[pl.ds(i, 128, stride=RANK), :].T
        w_ref[i, 0:RANK, :] = block[0:RANK]
        w_ref[i, RANK:128, :] = jnp.where(place == i, 1.0, 0.0).astype(F32)
        return carry

    lax.fori_loop(0, RANK, body, 0, unroll=4)


def eliminate(w_ref):
    for band in range(16):
        q = band // 2
        lo, hi = 8 * q, RANK + 8 * (q + 1)
        first = 4 * band
        rows = tuple(w_ref[first + a, lo:hi, :] for a in range(4))

        def step(k, rows):
            src = w_ref[k, lo:hi, :]
            return tuple(
                rows[a] - w_ref[k, first + a : first + a + 1, :] * src for a in range(4)
            )

        if first > 0:
            rows = lax.fori_loop(0, first, step, rows, unroll=2)
        rows = list(rows)
        for a in range(4):
            at = first + a - lo
            for b in range(a):
                rows[a] = rows[a] - rows[b][at : at + 1] * rows[b]
            pivot = rows[a][at : at + 1]
            scale = lax.rsqrt(pivot)
            scale = scale * (1.5 - 0.5 * pivot * scale * scale)
            rows[a] = rows[a] * scale
            w_ref[first + a, lo:hi, :] = rows[a]


def clear_lower(w_ref):
    place = lax.broadcasted_iota(jnp.int32, (RANK, 128), 0)

    def body(i, carry):
        w_ref[i, 0:RANK, :] = jnp.where(place >= i, w_ref[i, 0:RANK, :], 0.0)
        return carry

    lax.fori_loop(0, RANK, body, 0, unroll=4)


def store_lanes(w_ref, um_ref, amount):
    def body(i, carry):
        block = w_ref[i].T
        um_ref[pl.ds(i, amount, stride=RANK), :] = block[0:amount]
        return carry

    lax.fori_loop(0, RANK, body, 0, unroll=4)


def gram_kernel(v_ref, e_ref, g_ref, c_ref):
    def leaf(b, carry):
        v = v_ref[b]
        g_ref[pl.ds(b * RANK, RANK), 0:RANK] = exact(v, v, NT)
        return carry

    lax.fori_loop(0, LEAF, leaf, 0, unroll=4)

    def parent(p, carry):
        a = 2 * (p - LEAF)
        ea, eb = e_ref[a], e_ref[a + 1]
        ga = g_ref[pl.ds(a * RANK, RANK), 0:RANK]
        gb = g_ref[pl.ds((a + 1) * RANK, RANK), 0:RANK]
        both = jnp.concatenate([exact(ga, ea, NN), exact(gb, eb, NN)], axis=0)
        g_ref[pl.ds(p * RANK, RANK), 0:RANK] = exact(
            jnp.concatenate([ea, eb], axis=0), both, TN
        )
        return carry

    start, amount = LEAF, LEAF // 2
    while amount >= 1:
        lax.fori_loop(start, start + amount, parent, 0, unroll=min(amount, 4))
        start, amount = start + amount, amount // 2
    root = e_ref[NODES - 1]
    top = exact(root, exact(g_ref[(NODES - 1) * RANK : NODES * RANK, 0:RANK], root, NN), TN)
    c_ref[:, 0:RANK] = top[0:32]
    c_ref[:, RANK:128] = top[32:64]
    g_ref[NODES * RANK :, :] = jnp.zeros_like(g_ref[NODES * RANK :, :])


def gram_call(v, e):
    return pl.pallas_call(
        gram_kernel,
        out_shape=(
            jax.ShapeDtypeStruct((128 * RANK, 128), F32),
            jax.ShapeDtypeStruct((32, 128), F32),
        ),
        compiler_params=params(),
        cost_estimate=pl.CostEstimate(flops=400_000_000, bytes_accessed=8_000_000, transcendentals=0),
        name="gram_up",
    )(v, e)


def factor_kernel(g_ref, um_ref, unit_ref, w_ref):
    load_lanes(g_ref, w_ref)
    eliminate(w_ref)
    clear_lower(w_ref)
    place = lax.broadcasted_iota(jnp.int32, (RANK, 128), 0)
    rows = w_ref.reshape(RANK * 128, 128)

    def pack(i, diag):
        upper = w_ref[i, 0:RANK, :]
        lower = rows[pl.ds(i, RANK, stride=128), :]
        other = pltpu.roll(lower, 128 - 2 * QUART, axis=1)
        mixed = jnp.where(place >= i, upper, other)
        both = jnp.concatenate([mixed, pltpu.roll(mixed, 128 - QUART, axis=1)], axis=0).T
        unit_ref[pl.ds(i, QUART, stride=RANK), :] = both[0:QUART]
        return jnp.where(place == i, lower, diag)

    diag = lax.fori_loop(0, RANK, pack, jnp.zeros((RANK, 128), F32), unroll=4)
    unit_ref[QUART * RANK :, :] = jnp.concatenate([diag, diag], axis=0).T[0:RANK]
    store_lanes(w_ref, um_ref, RANK)


def factor_call(g):
    return pl.pallas_call(
        factor_kernel,
        out_shape=(
            jax.ShapeDtypeStruct((RANK * RANK, 128), F32),
            jax.ShapeDtypeStruct((UNIT * RANK, 128), F32),
        ),
        scratch_shapes=[pltpu.VMEM((RANK, 128, 128), F32)],
        compiler_params=params(),
        cost_estimate=pl.CostEstimate(flops=400_000_000, bytes_accessed=8_000_000, transcendentals=0),
        name="factor_local",
    )(g)


def apply_kernel(um_ref, v_ref, e_ref, leaves_ref, moved_ref):
    def leaf(b, carry):
        m = um_ref[b, :, RANK:128]
        leaves_ref[b] = mul3(m, v_ref[b], NN)
        return carry

    lax.fori_loop(0, LEAF, leaf, 0, unroll=2)

    def parent(p, carry):
        a = 2 * (p - LEAF)
        pa = mul3(um_ref[a, :, 0:RANK], e_ref[a], NN)
        pb = mul3(um_ref[a + 1, :, 0:RANK], e_ref[a + 1], NN)
        q = mul3(jnp.concatenate([pa, pb], axis=0), um_ref[p, :, RANK:128], NT)
        moved_ref[a] = q[0:RANK]
        moved_ref[a + 1] = q[RANK:128]
        return carry

    lax.fori_loop(LEAF, NODES, parent, 0, unroll=2)
    moved_ref[NODES - 1] = mul3(um_ref[NODES - 1, :, 0:RANK], e_ref[NODES - 1], NN)


def apply_call(um, v, e):
    return pl.pallas_call(
        apply_kernel,
        out_shape=(
            jax.ShapeDtypeStruct(v.shape, F32),
            jax.ShapeDtypeStruct(e.shape, F32),
        ),
        compiler_params=params(),
        cost_estimate=pl.CostEstimate(flops=600_000_000, bytes_accessed=20_000_000, transcendentals=0),
        name="apply_local",
    )(um, v, e)


def top_kernel(own_ref, c_ref, e_ref, p_ref, new_ref, root_ref, mine_ref, g_ref, w_ref, um_ref):
    def wide(d):
        x = c_ref[d]
        return jnp.concatenate([x[:, 0:RANK], x[:, RANK:128]], axis=0)

    def first(p, carry):
        g_ref[pl.ds((63 + p) * RANK, RANK), 0:RANK] = wide(2 * p) + wide(2 * p + 1)
        return carry

    lax.fori_loop(0, 64, first, 0, unroll=4)

    def join(n, carry):
        c = 2 * n + 1
        ea, eb = e_ref[c - 1], e_ref[c]
        ga = g_ref[pl.ds(c * RANK, RANK), 0:RANK]
        gb = g_ref[pl.ds((c + 1) * RANK, RANK), 0:RANK]
        both = jnp.concatenate([exact(ga, ea, NN), exact(gb, eb, NN)], axis=0)
        g_ref[pl.ds(n * RANK, RANK), 0:RANK] = exact(
            jnp.concatenate([ea, eb], axis=0), both, TN
        )
        return carry

    for level in range(5, -1, -1):
        begin = 2**level - 1
        lax.fori_loop(begin, 2 * begin + 1, join, 0, unroll=min(2**level, 4))
    g_ref[TOPN * RANK :, :] = jnp.zeros_like(g_ref[TOPN * RANK :, :])
    load_lanes(g_ref, w_ref)
    eliminate(w_ref)
    clear_lower(w_ref)
    store_lanes(w_ref, um_ref, 128)

    def out(n, carry):
        c = 2 * n + 1
        pa = mul3(um_ref[pl.ds(c * RANK, RANK), 0:RANK], e_ref[c - 1], NN)
        pb = mul3(um_ref[pl.ds((c + 1) * RANK, RANK), 0:RANK], e_ref[c], NN)
        m = um_ref[pl.ds(n * RANK, RANK), RANK:128]
        q = mul3(jnp.concatenate([pa, pb], axis=0), m, NT)
        new_ref[c - 1] = q[0:RANK]
        new_ref[c] = q[RANK:128]
        return carry

    lax.fori_loop(0, 63, out, 0, unroll=3)
    root_ref[...] = um_ref[0:RANK, 0:RANK]
    up = 63 + own_ref[0] // 2
    mine_ref[...] = mul3(p_ref[...], um_ref[pl.ds(pl.multiple_of(up * RANK, RANK), RANK), RANK:128], NT)


def top_call(own, c, e, p):
    vm = pl.BlockSpec(memory_space=pltpu.VMEM)
    return pl.pallas_call(
        top_kernel,
        in_specs=[pl.BlockSpec(memory_space=pltpu.SMEM), vm, vm, vm],
        out_shape=(
            jax.ShapeDtypeStruct(e.shape, F32),
            jax.ShapeDtypeStruct((RANK, RANK), F32),
            jax.ShapeDtypeStruct((RANK, RANK), F32),
        ),
        scratch_shapes=[
            pltpu.VMEM((128 * RANK, 128), F32),
            pltpu.VMEM((RANK, 128, 128), F32),
            pltpu.VMEM((128 * RANK, 128), F32),
        ],
        compiler_params=params(),
        cost_estimate=pl.CostEstimate(flops=1_000_000_000, bytes_accessed=60_000_000, transcendentals=0),
        name="top_tree",
    )(own, c, e, p)


def couple_kernel(where_ref, s_ref, um_ref, win_ref, out_ref):
    row = pl.program_id(0)
    down = lax.broadcasted_iota(jnp.int32, (RANK, RANK), 0)
    over = lax.broadcasted_iota(jnp.int32, (RANK, RANK), 1)
    parts = []
    for c in range(CPL):
        code = where_ref[row, c]
        unit = code // 64
        local = code % 64
        quarter = local // QUART
        x = win_ref[unit * UNIT + local % QUART]
        half = quarter % 2
        plain = jnp.where(half == 0, x[:, 0:RANK], x[:, RANK:128])
        t = x.T
        turned = jnp.where(half == 0, t[0:RANK], t[RANK:128])
        diag = win_ref[unit * UNIT + QUART, pl.ds(local, 1), 0:RANK]
        second = quarter >= 2
        strict = jnp.where(second, plain, turned)
        on = jnp.where(second, jnp.broadcast_to(diag, (RANK, RANK)), turned)
        lower = jnp.where(down > over, strict, jnp.where(down == over, on, 0.0))
        parts.append(mul3(s_ref[0, c], lower, NN))
    u = split(um_ref[row, :, 0:RANK])
    for c in range(CPL):
        out_ref[0, c] = three(u, split(parts[c]), NN)


def couple_call(where, s, um, win):
    return pl.pallas_call(
        couple_kernel,
        grid_spec=pltpu.PrefetchScalarGridSpec(
            num_scalar_prefetch=1,
            grid=(ROW,),
            in_specs=[
                pl.BlockSpec((1, CPL, RANK, RANK), lambda r, w: (r, 0, 0, 0)),
                pl.BlockSpec(memory_space=pltpu.VMEM),
                pl.BlockSpec(memory_space=pltpu.VMEM),
            ],
            out_specs=pl.BlockSpec((1, CPL, RANK, RANK), lambda r, w: (r, 0, 0, 0)),
        ),
        out_shape=jax.ShapeDtypeStruct(s.shape, F32),
        compiler_params=params(),
        cost_estimate=pl.CostEstimate(flops=1_500_000_000, bytes_accessed=45_000_000, transcendentals=0),
        name="couple",
    )(where, s, um, win)


def shifted(array, axis, by):
    devices = lax.axis_size(axis)
    pairs = [(i, i + by) for i in range(devices) if 0 <= i + by < devices]
    return lax.ppermute(array, axis, pairs)


def on_device(leaf_bases, transfers, top_transfers, couplings, coupling_cols):
    devices = lax.axis_size("leaf")
    own = lax.axis_index("leaf").astype(jnp.int32)
    grams, carried = gram_call(leaf_bases, transfers)
    frontier = lax.all_gather(carried, "leaf", axis=0, tiled=False)
    um, unit = factor_call(grams)
    um = um.reshape(RANK, RANK, 128)
    unit = unit.reshape(UNIT, RANK, 128)
    trio = jnp.concatenate([shifted(unit, "leaf", COLUMN), unit, shifted(unit, "leaf", -COLUMN)], axis=0)
    groups = [[c * COLUMN + j for j in range(COLUMN)] for c in range(devices // COLUMN)]
    window = lax.all_gather(trio, "leaf", axis_index_groups=groups, axis=0, tiled=True)
    device_of = coupling_cols // ROW
    side = device_of // COLUMN - own // COLUMN + 1
    where = (device_of % COLUMN * 3 + side) * 64 + coupling_cols % ROW
    new_leaves, moved = apply_call(um, leaf_bases, transfers)
    new_top, root_factor, mine = top_call(
        own.reshape(1), frontier, top_transfers, moved[NODES - 1]
    )
    new_transfers = moved.at[NODES - 1].set(mine)
    new_couplings = couple_call(where, couplings, um, window)
    return (new_leaves, new_transfers, new_top, root_factor, new_couplings)


def solution(mesh):
    in_specs = (
        P("leaf", None, None),
        P("leaf", None, None),
        P(),
        P("leaf", None, None, None),
        P("leaf", None),
    )
    out_specs = (
        P("leaf", None, None),
        P("leaf", None, None),
        P(),
        P(),
        P("leaf", None, None, None),
    )
    return jax.shard_map(
        on_device, mesh=mesh, in_specs=in_specs, out_specs=out_specs, check_vma=False
    )
```

time: 2440 us -> 228 us (0.09); the launches traced: 2400 us -> 224 us
  other arithmetic: 1700 us -> 60.9 us
  waiting for transfers between devices: 289 us -> 18.3 us
  local copies, waits for them, and re-layouts: 187 us -> 15.9 us
  matrix products: 130 us -> 0 us
  Pallas kernels: 0 us -> 109 us
  starting transfers between devices: 76.9 us -> 5.54 us
    another operation x74 -> x0, other arithmetic: 1680 us -> none  [the longest x36 939 us: join_pairs(): factor = jnp.linalg.cholesky(gram_matrix)]
    ppermute x16 -> x2, waiting for transfers between devices: 289 us -> 13.9 us  [shifted(): return lax.ppermute(array, axis, pairs)]
    dot_general x52 -> x0, matrix products: 113 us -> none  [the longest x1 22.9 us: on_device(): jnp.einsum('rcil,rclj->rcij', left_side, column_factor, precision=PRECISE)]
    pallas_call x0 -> x4, Pallas kernels: none -> 109 us  [the longest x1 55.1 us: couple_call(): pl.pallas_call(couple_kernel, grid_spec=pltpu.PrefetchScalarGridSpec(num_...]
    ppermute x16 -> x2, starting transfers between devices: 76.8 us -> 5.46 us  [shifted(): return lax.ppermute(array, axis, pairs)]
    pallas_call x0 -> x1, other arithmetic: none -> 59.6 us  [top_call(): pl.pallas_call(top_kernel, in_specs=[pl.BlockSpec(memory_space=pltpu.SMEM...]
    unnamed x138 -> x11, local copies, waits for them, and re-layouts: 73.5 us -> 15.2 us
    another operation x28 -> x0, local copies, waits for them, and re-layouts: 35.4 us -> none  [the longest x22 21.6 us: pair_order(): jnp.stack([lower_q, upper_q], axis=1).reshape((-1,) + lower_q.shape[1:])]
  transfers between devices with their start and end apart: 17 -> 4, of which waited for: 8 -> 4; matrix products, arithmetic and copies ran while one was open for 18% -> 32% of each run, Pallas kernels for 0% -> 17%
where the time goes in v1:
time: 228 us; the launch traced here: 224 us
  Pallas kernels  109 us (48%)
  other arithmetic  60.9 us (27%)
  waiting for transfers between devices  18.3 us (8%)
  local copies, waits for them, and re-layouts  15.9 us (7%)
  between operations  14.1 us (6%)
  starting transfers between devices  5.54 us (2%)
    pallas_call x1, other arithmetic, top_call(): pl.pallas_call(top_kernel, in_specs=[pl.BlockSpec(memory_space=pltpu.SMEM...  59.6 us
    pallas_call x1, Pallas kernels, couple_call(): pl.pallas_call(couple_kernel, grid_spec=pltpu.PrefetchScalarGridSpec(num_...  55.1 us
    pallas_call x1, Pallas kernels, factor_call(): pl.pallas_call(factor_kernel, out_shape=(jax.ShapeDtypeStruct((RANK * RAN...  22.2 us
    pallas_call x1, Pallas kernels, gram_call(): pl.pallas_call(gram_kernel, out_shape=(jax.ShapeDtypeStruct((128 * RANK,...  16.7 us
    pallas_call x1, Pallas kernels, apply_call(): pl.pallas_call(apply_kernel, out_shape=(jax.ShapeDtypeStruct(v.shape, F32...  15.4 us
    unnamed x11, local copies, waits for them, and re-layouts  15.2 us
    ppermute x2, waiting for transfers between devices, shifted(): return lax.ppermute(array, axis, pairs)  13.9 us
    ppermute x2, starting transfers between devices, shifted(): return lax.ppermute(array, axis, pairs)  5.46 us
  transfers between devices with their start and end apart: 4, of which 4 were waited for; matrix products, arithmetic and copies ran while one was open for 32% of the time, Pallas kernels for 17%

profile of v1, /device:TPU:7, one launch (start us, length us, event | category | flops | bytes accessed | tf_op | source)
XLA Modules:
  0.0 224.1 jit_solution(5142496050903383375)
XLA Ops:
  7.2 0.0 all-gather.6.cloned.1.call-start
  7.2 0.0 copy-start
  7.2 1.6 copy-done
  8.8 0.0 copy-start.1
  8.8 1.6 copy-done.1
  10.4 16.7 %gram_up.1 = (f32[8192,128]{1,0:T(8,128)}, f32[32,128]{1,0:T(8,128)}) custom-call(f32[32,64,256]{2,1,0:T(8,128)S(1)} %copy-done, f32[63,64,64]{2,1,0:T(8,128)S(1)} %copy-done.1), custom_call_target="tpu_custom_call" | custom-call | flops 400000000 | bytes 8000000 | tf_op jit(solution)/shard_map/gram_up/pallas_call | solution.py:142
  27.1 0.0 all-gather.6.cloned.1.call-update
  27.1 0.0 all-gather.4.cloned.1.call-start
  27.1 22.2 %factor_local.1 = (f32[4096,128]{1,0:T(8,128)S(1)}, f32[960,128]{1,0:T(8,128)S(1)}) custom-call(f32[8192,128]{1,0:T(8,128)} %get-tuple-element.26.g_ref), custom_call_target="tpu_custom_call" | custom-call | flops 400000000 | bytes 8000000 | tf_op jit(solution)/shard_map/factor_local/pallas_call | solution.py:176
  49.4 0.0 copy-start.3
  49.4 3.1 %collective-permute-start = (f32[15,64,128]{2,1,0:T(8,128)S(1)}, f32[15,64,128]{2,1,0:T(8,128)S(1)}, u32[]{:S(2)}, u32[]{:S(2)}) collective-permute-start(f32[15,64,128]{2,1,0:T(8,128)S(1)} %bitcast.10), channel_id=1, source_target_pairs={{0,8},{1,9},{2,10},{3,11},{4,12},{5,13},{6,14},{7,15},{8,16},{9,17... | collective-permute-start | bytes 1474568 | tf_op jit(solution)/shard_map/ppermute | solution.py:340
  52.5 2.3 %collective-permute-start.1 = (f32[15,64,128]{2,1,0:T(8,128)S(1)}, f32[15,64,128]{2,1,0:T(8,128)S(1)}, u32[]{:S(2)}, u32[]{:S(2)}) collective-permute-start(f32[15,64,128]{2,1,0:T(8,128)S(1)} %bitcast.11), channel_id=1, source_target_pairs={{8,0},{9,1},{10,2},{11,3},{12,4},{13,5},{14,6},{15,7},{16,8},{17,9... | collective-permute-start | bytes 1474568 | tf_op jit(solution)/shard_map/ppermute | solution.py:340
  54.8 8.8 %collective-permute-done = f32[15,64,128]{2,1,0:T(8,128)S(1)} collective-permute-done((f32[15,64,128]{2,1,0:T(8,128)S(1)}, f32[15,64,128]{2,1,0:T(8,128)S(1)}, u32[]{:S(2)}, u32[]{:S(2)}) %collective-permute-start) | collective-permute-done | bytes 491552 | tf_op jit(solution)/shard_map/ppermute | solution.py:340
  63.7 5.0 %collective-permute-done.1 = f32[15,64,128]{2,1,0:T(8,128)S(1)} collective-permute-done((f32[15,64,128]{2,1,0:T(8,128)S(1)}, f32[15,64,128]{2,1,0:T(8,128)S(1)}, u32[]{:S(2)}, u32[]{:S(2)}) %collective-permute-start.1) | collective-permute-done | bytes 491552 | tf_op jit(solution)/shard_map/ppermute | solution.py:340
  68.7 1.2 pad_maximum_fusion
  69.9 0.0 all-gather.4.cloned.1.call-update
  70.0 0.0 copy-done.3
  70.0 0.1 copy.16
  70.1 5.5 %copy.15 = f32[126,64,64]{2,1,0:T(8,128)} copy(f32[126,64,64]{0,2,1:T(8,128)} %param.9) | data formatting | bytes 4128768 | tf_op args[2]
  75.6 0.0 copy-start.2
  75.6 1.6 copy-done.2
  77.2 15.4 %apply_local.1 = (f32[32,64,256]{2,1,0:T(8,128)}, f32[63,64,64]{2,1,0:T(8,128)}) custom-call(f32[64,64,128]{2,1,0:T(8,128)S(1)} %bitcast.8, f32[32,64,256]{2,1,0:T(8,128)} %v_ref.3, f32[63,64,64]{2,1,0:T(8,128)S(1)} %copy-done.2), custom_call_target="tpu_custom_call" | custom-call | flops 600000000 | bytes 20000000 | tf_op jit(solution)/shard_map/apply_local/pallas_call | solution.py:211
  92.6 0.1 fusion.3.where_ref
  92.6 0.8 slice_bitcast_fusion
  93.4 3.6 %all-gather.6.cloned.1.call-done = f32[4096,128]{1,0:T(8,128)} async-done(((f32[32,128]{1,0:T(8,128)}), f32[4096,128]{1,0:T(8,128)}) %all-gather.6.cloned.1.call-update) | async-done | bytes 2097168 | tf_op jit(solution)/shard_map/all_gather | solution.py:347
  97.0 59.6 %top_tree.1 = (f32[63,64,64]{2,1,0:T(8,128)}, f32[126,64,64]{2,1,0:T(8,128)}, f32[64,64]{1,0:T(8,128)}) fusion(f32[63,64,64]{2,1,0:T(8,128)} %get-tuple-element.29, s32[1]{0:T(128)} %bitcast.1, f32[128,32,128]{2,1,0:T(8,128)} %bitcast.13, f32[126,64,64]{2,1,0:T(8,128)} %copy.15, f32[64,64]{1,0:T(8,128)S(1)} %slice_bitcast_fusion), kind=kCustom, calls=%fused_computation.8 | custom fusion | flops 1000000000 | bytes 10437120 | tf_op jit(solution)/shard_map/top_tree/pallas_call | solution.py:272
  156.7 4.8 %copy.19 = f32[126,64,64]{0,2,1:T(8,128)} copy(f32[126,64,64]{2,1,0:T(8,128)} %get-tuple-element.48) | data formatting | bytes 4128768
  161.5 0.7 all-gather.4.cloned.1.call-done.win_ref
  162.2 55.1 %couple.1 = f32[56,8,64,64]{3,2,1,0:T(8,128)} custom-call(s32[56,8]{1,0:T(8,128)S(1)} %fusion.3.where_ref, f32[56,8,64,64]{3,2,1,0:T(8,128)} %s_ref.1, f32[64,64,128]{2,1,0:T(8,128)S(1)} %bitcast.9, f32[360,64,128]{2,1,0:T(8,128)} %all-gather.4.cloned.1.call-done.win_ref), custom_call_target="tpu_custom_call" | custom-call | flops 1500000000 | bytes 45000000 | tf_op jit(solution)/shard_map/couple/pallas_call | solution.py:318
Async XLA Ops:
  7.2 89.9 %all-gather.6.cloned.1.call-start = ((), (), s32[]{:S(2)}) async-start(), calls=%async_computation.1 | async-start | bytes 2113536 | tf_op jit(solution)/shard_map/all_gather | solution.py:347
  7.2 1.6 copy-start
  8.8 1.6 copy-start.1
  27.1 135.1 %all-gather.4.cloned.1.call-start = ((), (), s32[]{:S(2)}) async-start(), calls=%async_computation | async-start | bytes 13271040 | tf_op jit(solution)/shard_map/all_gather | solution.py:353
  49.4 20.6 %copy-start.3 = (s32[56,8]{0,1:T(8,128)S(1)}, s32[56,8]{0,1:T(8,128)}, u32[]{:S(2)}) copy-start(s32[56,8]{0,1:T(8,128)} %param.11) | copy-start | bytes 5380
  49.4 14.3 %collective-permute-start = (f32[15,64,128]{2,1,0:T(8,128)S(1)}, f32[15,64,128]{2,1,0:T(8,128)S(1)}, u32[]{:S(2)}, u32[]{:S(2)}) collective-permute-start(f32[15,64,128]{2,1,0:T(8,128)S(1)} %bitcast.10), channel_id=1, source_target_pairs={{0,8},{1,9},{2,10},{3,11},{4,12},{5,13},{6,14},{7,15},{8,16},{9,17... | collective-permute-start | bytes 1474568 | tf_op jit(solution)/shard_map/ppermute | solution.py:340
  52.5 16.2 %collective-permute-start.1 = (f32[15,64,128]{2,1,0:T(8,128)S(1)}, f32[15,64,128]{2,1,0:T(8,128)S(1)}, u32[]{:S(2)}, u32[]{:S(2)}) collective-permute-start(f32[15,64,128]{2,1,0:T(8,128)S(1)} %bitcast.11), channel_id=1, source_target_pairs={{8,0},{9,1},{10,2},{11,3},{12,4},{13,5},{14,6},{15,7},{16,8},{17,9... | collective-permute-start | bytes 1474568 | tf_op jit(solution)/shard_map/ppermute | solution.py:340
  75.6 1.6 copy-start.2
Sparse Core Ops, SparseCore 0:
  27.2 69.7 all-gather.5
  98.7 63.4 all-gather.3

commit v2 on v1

v2 whole, which is shorter than its diff:
```python
import functools

import jax
import jax.numpy as jnp
from jax import lax
from jax.experimental import pallas as pl
from jax.experimental.pallas import tpu as pltpu
from jax.sharding import PartitionSpec as P

RANK = 64
LEAF = 32
NODES = 63
ROW = 56
CPL = 8
QUART = 14
UNIT = QUART + 1
COLUMN = 8
TOPN = 127
ROWS_STEP = 8
VMEM_LIMIT = 48 * 1024 * 1024
F32 = jnp.float32
BF16 = jnp.bfloat16
FULL = lax.Precision.HIGHEST

NN = (((1,), (0,)), ((), ()))
NT = (((1,), (1,)), ((), ()))
TN = (((0,), (0,)), ((), ()))


def exact(a, b, dims):
    return lax.dot_general(a, b, dims, precision=FULL, preferred_element_type=F32)


def split(a):
    high = a.astype(BF16)
    return high, (a - high.astype(F32)).astype(BF16)


def three(a, b, dims):
    ah, al = a
    bh, bl = b
    dot = functools.partial(lax.dot_general, dimension_numbers=dims, preferred_element_type=F32)
    return dot(ah, bh) + (dot(ah, bl) + dot(al, bh))


def mul3(a, b, dims):
    return three(split(a), split(b), dims)


def cost(us):
    return pl.CostEstimate(flops=us * 1_000_000, bytes_accessed=us * 2_500_000, transcendentals=0)


def params():
    return pltpu.CompilerParams(vmem_limit_bytes=VMEM_LIMIT)


def load_lanes(g_ref, w_ref):
    place = lax.broadcasted_iota(jnp.int32, (RANK, 128), 0)

    def body(i, carry):
        block = g_ref[pl.ds(i, 128, stride=RANK), :].T
        w_ref[i, 0:RANK, :] = block[0:RANK]
        w_ref[i, RANK:128, :] = jnp.where(place == i, 1.0, 0.0).astype(F32)
        return carry

    lax.fori_loop(0, RANK, body, 0, unroll=8)


def eliminate(w_ref):
    for band in range(16):
        q = band // 2
        lo, hi = 8 * q, RANK + 8 * (q + 1)
        first = 4 * band
        rows = tuple(w_ref[first + a, lo:hi, :] for a in range(4))

        def step(k, rows):
            src = w_ref[k, lo:hi, :]
            return tuple(
                rows[a] - w_ref[k, first + a : first + a + 1, :] * src for a in range(4)
            )

        if first > 0:
            rows = lax.fori_loop(0, first, step, rows, unroll=4)
        rows = list(rows)
        for a in range(4):
            at = first + a - lo
            for b in range(a):
                rows[a] = rows[a] - rows[b][at : at + 1] * rows[b]
            pivot = rows[a][at : at + 1]
            scale = lax.rsqrt(pivot)
            scale = scale * (1.5 - 0.5 * pivot * scale * scale)
            rows[a] = rows[a] * scale
            w_ref[first + a, lo:hi, :] = rows[a]


def store_lanes(w_ref, um_ref, amount):
    place = lax.broadcasted_iota(jnp.int32, (RANK, 128), 0)

    def body(i, carry):
        upper = jnp.where(place >= i, w_ref[i, 0:RANK, :], 0.0)
        block = jnp.concatenate([upper, w_ref[i, RANK:128, :]], axis=0).T
        um_ref[pl.ds(i, amount, stride=RANK), :] = block[0:amount]
        return carry

    lax.fori_loop(0, RANK, body, 0, unroll=8)


def block_at(n):
    return pl.ds(pl.multiple_of(n * RANK, RANK), RANK)


def gram_kernel(v_ref, e_ref, g_ref, c_ref):
    def leaf(b, carry):
        v = v_ref[b]
        g_ref[block_at(b), 0:RANK] = exact(v, v, NT)
        return carry

    lax.fori_loop(0, LEAF, leaf, 0, unroll=8)

    def parent(p, carry):
        a = 2 * (p - LEAF)
        ea, eb = e_ref[a], e_ref[a + 1]
        ga = g_ref[block_at(a), 0:RANK]
        gb = g_ref[block_at(a + 1), 0:RANK]
        both = jnp.concatenate([exact(ga, ea, NN), exact(gb, eb, NN)], axis=0)
        g_ref[block_at(p), 0:RANK] = exact(
            jnp.concatenate([ea, eb], axis=0), both, TN
        )
        return carry

    start, amount = LEAF, LEAF // 2
    while amount >= 1:
        lax.fori_loop(start, start + amount, parent, 0, unroll=min(amount, 16))
        start, amount = start + amount, amount // 2
    root = e_ref[NODES - 1]
    top = exact(root, exact(g_ref[(NODES - 1) * RANK : NODES * RANK, 0:RANK], root, NN), TN)
    c_ref[:, 0:RANK] = top[0:32]
    c_ref[:, RANK:128] = top[32:64]
    g_ref[NODES * RANK :, :] = jnp.zeros_like(g_ref[NODES * RANK :, :])


def gram_call(v, e):
    return pl.pallas_call(
        gram_kernel,
        out_shape=(
            jax.ShapeDtypeStruct((128 * RANK, 128), F32),
            jax.ShapeDtypeStruct((32, 128), F32),
        ),
        compiler_params=params(),
        cost_estimate=cost(12),
        name="gram_up",
    )(v, e)


def factor_kernel(g_ref, w_ref, unit_ref):
    load_lanes(g_ref, w_ref)
    eliminate(w_ref)
    place = lax.broadcasted_iota(jnp.int32, (RANK, 128), 0)
    rows = w_ref.reshape(RANK * 128, 128)

    def pack(i, diag):
        upper = w_ref[i, 0:RANK, :]
        lower = rows[pl.ds(i, RANK, stride=128), :]
        other = pltpu.roll(lower, 128 - 2 * QUART, axis=1)
        mixed = jnp.where(place >= i, upper, other)
        both = jnp.concatenate([mixed, pltpu.roll(mixed, 128 - QUART, axis=1)], axis=0).T
        unit_ref[pl.ds(i, QUART, stride=RANK), :] = both[0:QUART]
        return jnp.where(place == i, lower, diag)

    diag = lax.fori_loop(0, RANK, pack, jnp.zeros((RANK, 128), F32), unroll=8)
    unit_ref[QUART * RANK :, :] = jnp.concatenate([diag, diag], axis=0).T[0:RANK]


def factor_call(g):
    return pl.pallas_call(
        factor_kernel,
        out_shape=(
            jax.ShapeDtypeStruct((RANK, 128, 128), F32),
            jax.ShapeDtypeStruct((UNIT * RANK, 128), F32),
        ),
        compiler_params=params(),
        cost_estimate=cost(15),
        name="factor_local",
    )(g)


def turn_kernel(w_ref, um_ref):
    store_lanes(w_ref, um_ref, RANK)


def turn_call(w):
    return pl.pallas_call(
        turn_kernel,
        out_shape=jax.ShapeDtypeStruct((RANK * RANK, 128), F32),
        compiler_params=params(),
        cost_estimate=cost(6),
        name="turn_local",
    )(w)


def apply_kernel(um_ref, v_ref, e_ref, leaves_ref, moved_ref):
    def leaf(b, carry):
        m = um_ref[b, :, RANK:128]
        leaves_ref[b] = mul3(m, v_ref[b], NN)
        return carry

    lax.fori_loop(0, LEAF, leaf, 0, unroll=8)

    def parent(p, carry):
        a = 2 * (p - LEAF)
        pa = mul3(um_ref[a, :, 0:RANK], e_ref[a], NN)
        pb = mul3(um_ref[a + 1, :, 0:RANK], e_ref[a + 1], NN)
        q = mul3(jnp.concatenate([pa, pb], axis=0), um_ref[p, :, RANK:128], NT)
        moved_ref[a] = q[0:RANK]
        moved_ref[a + 1] = q[RANK:128]
        return carry

    lax.fori_loop(LEAF, NODES - 1, parent, 0, unroll=10)
    parent(NODES - 1, 0)
    moved_ref[NODES - 1] = mul3(um_ref[NODES - 1, :, 0:RANK], e_ref[NODES - 1], NN)


def apply_call(um, v, e):
    return pl.pallas_call(
        apply_kernel,
        out_shape=(
            jax.ShapeDtypeStruct(v.shape, F32),
            jax.ShapeDtypeStruct(e.shape, F32),
        ),
        compiler_params=params(),
        cost_estimate=cost(9),
        name="apply_local",
    )(um, v, e)


def top_gram_kernel(c_ref, e_ref, w_ref, g_ref):
    def wide(d):
        x = c_ref[d]
        return jnp.concatenate([x[:, 0:RANK], x[:, RANK:128]], axis=0)

    def first(p, carry):
        g_ref[block_at(63 + p), 0:RANK] = wide(2 * p) + wide(2 * p + 1)
        return carry

    lax.fori_loop(0, 64, first, 0, unroll=16)

    def join(n, carry):
        c = 2 * n + 1
        ea, eb = e_ref[c - 1], e_ref[c]
        ga = g_ref[block_at(c), 0:RANK]
        gb = g_ref[block_at(c + 1), 0:RANK]
        both = jnp.concatenate([exact(ga, ea, NN), exact(gb, eb, NN)], axis=0)
        g_ref[block_at(n), 0:RANK] = exact(jnp.concatenate([ea, eb], axis=0), both, TN)
        return carry

    for level in range(5, -1, -1):
        begin = 2**level - 1
        lax.fori_loop(begin, 2 * begin + 1, join, 0, unroll=min(2**level, 16))
    g_ref[TOPN * RANK :, :] = jnp.zeros_like(g_ref[TOPN * RANK :, :])
    load_lanes(g_ref, w_ref)
    eliminate(w_ref)


def top_gram_call(c, e):
    return pl.pallas_call(
        top_gram_kernel,
        out_shape=jax.ShapeDtypeStruct((RANK, 128, 128), F32),
        scratch_shapes=[pltpu.VMEM((128 * RANK, 128), F32)],
        compiler_params=params(),
        cost_estimate=cost(25),
        name="top_gram",
    )(c, e)


def top_out_kernel(own_ref, w_ref, e_ref, p_ref, new_ref, root_ref, mine_ref, um_ref):
    store_lanes(w_ref, um_ref, 128)

    def out(n, carry):
        c = 2 * n + 1
        pa = mul3(um_ref[block_at(c), 0:RANK], e_ref[c - 1], NN)
        pb = mul3(um_ref[block_at(c + 1), 0:RANK], e_ref[c], NN)
        m = um_ref[block_at(n), RANK:128]
        q = mul3(jnp.concatenate([pa, pb], axis=0), m, NT)
        new_ref[c - 1] = q[0:RANK]
        new_ref[c] = q[RANK:128]
        return carry

    lax.fori_loop(0, 63, out, 0, unroll=9)
    root_ref[...] = um_ref[0:RANK, 0:RANK]
    up = 63 + own_ref[0] // 2
    mine_ref[...] = mul3(p_ref[...], um_ref[block_at(up), RANK:128], NT)


def top_out_call(own, w, e, p):
    vm = pl.BlockSpec(memory_space=pltpu.VMEM)
    return pl.pallas_call(
        top_out_kernel,
        in_specs=[pl.BlockSpec(memory_space=pltpu.SMEM), vm, vm, vm],
        out_shape=(
            jax.ShapeDtypeStruct(e.shape, F32),
            jax.ShapeDtypeStruct((RANK, RANK), F32),
            jax.ShapeDtypeStruct((RANK, RANK), F32),
        ),
        scratch_shapes=[pltpu.VMEM((128 * RANK, 128), F32)],
        compiler_params=params(),
        cost_estimate=cost(17),
        name="top_out",
    )(own, w, e, p)


def left_kernel(s_ref, um_ref, z_ref):
    first = pl.program_id(0) * ROWS_STEP

    def one(r, carry):
        u = split(um_ref[first + r, :, 0:RANK])
        for c in range(CPL):
            z = three(u, split(s_ref[r, c]), NN)
            high = z.astype(BF16).astype(F32)
            z_ref[r, c] = jnp.concatenate([high, z - high], axis=1).astype(BF16)
        return carry

    lax.fori_loop(0, ROWS_STEP, one, 0, unroll=4)


def left_call(s, um):
    return pl.pallas_call(
        left_kernel,
        grid=(ROW // ROWS_STEP,),
        in_specs=[
            pl.BlockSpec((ROWS_STEP, CPL, RANK, RANK), lambda r: (r, 0, 0, 0)),
            pl.BlockSpec(memory_space=pltpu.VMEM),
        ],
        out_specs=pl.BlockSpec((ROWS_STEP, CPL, RANK, 128), lambda r: (r, 0, 0, 0)),
        out_shape=jax.ShapeDtypeStruct((ROW, CPL, RANK, 128), BF16),
        compiler_params=params(),
        cost_estimate=cost(17),
        name="couple_left",
    )(s, um)


def right_kernel(where_ref, z_ref, a_ref, b_ref, c_ref, d_ref, out_ref, win_ref, sems):
    @pl.when(pl.program_id(0) == 0)
    def _():
        copies = []
        begin = 0
        for k, piece in enumerate((a_ref, b_ref, c_ref, d_ref)):
            amount = piece.shape[0]
            target = win_ref.at[pl.ds(begin, amount)]
            copies.append(pltpu.make_async_copy(piece, target, sems.at[k]))
            begin += amount
        for copy in copies:
            copy.start()
        for copy in copies:
            copy.wait()

    first = pl.program_id(0) * ROWS_STEP
    down = lax.broadcasted_iota(jnp.int32, (RANK, RANK), 0)
    over = lax.broadcasted_iota(jnp.int32, (RANK, RANK), 1)

    def one(r, carry):
        for c in range(CPL):
            code = where_ref[first + r, c]
            unit = code // 64
            local = code % 64
            quarter = local // QUART
            x = win_ref[unit * UNIT + local % QUART]
            plain = jnp.where(quarter % 2 == 0, x[:, 0:RANK], x[:, RANK:128])
            turned = plain.T
            diag = win_ref[unit * UNIT + QUART, pl.ds(local, 1), 0:RANK]
            second = quarter >= 2
            strict = jnp.where(second, plain, turned)
            on = jnp.where(second, jnp.broadcast_to(diag, (RANK, RANK)), turned)
            lower = jnp.where(down > over, strict, jnp.where(down == over, on, 0.0))
            high, low = split(lower)
            z = z_ref[r, c]
            dot = functools.partial(
                lax.dot_general, dimension_numbers=NN, preferred_element_type=F32
            )
            out_ref[r, c] = dot(z, jnp.concatenate([high, high], axis=0)) + dot(z[:, 0:RANK], low)
        return carry

    lax.fori_loop(0, ROWS_STEP, one, 0, unroll=4)


def right_call(where, z, pieces):
    return pl.pallas_call(
        right_kernel,
        grid_spec=pltpu.PrefetchScalarGridSpec(
            num_scalar_prefetch=1,
            grid=(ROW // ROWS_STEP,),
            in_specs=[
                pl.BlockSpec((ROWS_STEP, CPL, RANK, 128), lambda r, w: (r, 0, 0, 0)),
            ]
            + [pl.BlockSpec(memory_space=pl.ANY)] * 4,
            out_specs=pl.BlockSpec((ROWS_STEP, CPL, RANK, RANK), lambda r, w: (r, 0, 0, 0)),
            scratch_shapes=[
                pltpu.VMEM((3 * COLUMN * UNIT, RANK, 128), F32),
                pltpu.SemaphoreType.DMA((4,)),
            ],
        ),
        out_shape=jax.ShapeDtypeStruct((ROW, CPL, RANK, RANK), F32),
        compiler_params=params(),
        cost_estimate=cost(20),
        name="couple_right",
    )(where, z, *pieces)


def shifted(array, axis, by):
    devices = lax.axis_size(axis)
    pairs = [(i, i + by) for i in range(devices) if 0 <= i + by < devices]
    return lax.ppermute(array, axis, pairs)


def swapped(array):
    devices = lax.axis_size("leaf")
    return lax.ppermute(array, "leaf", [(i, i ^ 1) for i in range(devices)])


def turned_column(array, by):
    devices = lax.axis_size("leaf")
    pairs = [(i, i // COLUMN * COLUMN + (i % COLUMN + 2 * by) % COLUMN) for i in range(devices)]
    return lax.ppermute(array, "leaf", pairs)


def together(*values):
    return lax.optimization_barrier(values)


def on_device(leaf_bases, transfers, top_transfers, couplings, coupling_cols):
    own = lax.axis_index("leaf").astype(jnp.int32)
    device_of = coupling_cols // ROW
    side = device_of // COLUMN - own // COLUMN
    steps = (own % COLUMN // 2 - device_of % COLUMN // 2) % (COLUMN // 2)
    other = (device_of + own) % 2
    place = jnp.where(
        side == 0, 4 * other + steps, 8 + 8 * other + 2 * steps + (side > 0).astype(jnp.int32)
    )
    where = place * 64 + coupling_cols % ROW

    grams, carried = gram_call(leaf_bases, transfers)
    frontier = lax.all_gather(carried, "leaf", axis=0, tiled=False)
    wide, unit = factor_call(grams)
    unit = unit.reshape(UNIT, RANK, 128)
    before = shifted(unit, "leaf", COLUMN)
    after = shifted(unit, "leaf", -COLUMN)
    line = [unit] + [turned_column(unit, by) for by in (1, 2, 3)]
    um = turn_call(wide).reshape(RANK, RANK, 128)
    new_leaves, moved = apply_call(um, leaf_bases, transfers)
    moved, um, before, after, *line = together(moved, um, before, after, *line)

    near = jnp.concatenate(line, axis=0)
    near_other = swapped(near)
    pair = jnp.concatenate([before, after], axis=0)
    sides = [pair] + [turned_column(pair, by) for by in (1, 2, 3)]
    left = left_call(couplings, um)
    left, near_other, frontier = together(left, near_other, frontier)

    top_wide = top_gram_call(frontier, top_transfers)
    top_wide, left, *sides = together(top_wide, left, *sides)
    far = jnp.concatenate(sides, axis=0)
    far_other = swapped(far)
    new_top, root_factor, mine = top_out_call(
        own.reshape(1), top_wide, top_transfers, moved[NODES - 1]
    )
    new_transfers = moved.at[NODES - 1].set(mine)
    new_couplings = right_call(where, left, (near, near_other, far, far_other))
    return (new_leaves, new_transfers, new_top, root_factor, new_couplings)


def solution(mesh):
    in_specs = (
        P("leaf", None, None),
        P("leaf", None, None),
        P(),
        P("leaf", None, None, None),
        P("leaf", None),
    )
    out_specs = (
        P("leaf", None, None),
        P("leaf", None, None),
        P(),
        P(),
        P("leaf", None, None, None),
    )
    return jax.shard_map(
        on_device, mesh=mesh, in_specs=in_specs, out_specs=out_specs, check_vma=False
    )
```

time: 228 us -> 219 us (0.961)
  other arithmetic: 60.9 us -> 15.1 us
  waiting for transfers between devices: 18.3 us -> 35.2 us
  local copies, waits for them, and re-layouts: 15.9 us -> 31.5 us
  starting transfers between devices: 5.54 us -> 14.6 us
  Pallas kernels: 109 us -> 106 us
    pallas_call x1, other arithmetic: 59.6 us -> 15 us  [top_out_call(): pl.pallas_call(top_out_kernel, in_specs=[pl.BlockSpec(memory_space=pltpu....]
    all_gather x1, waiting for transfers between devices: 3.64 us -> 31 us  [on_device(): frontier = lax.all_gather(carried, 'leaf', axis=0, tiled=False)]
    ppermute x2, waiting for transfers between devices: 13.9 us -> 0.01 us  [shifted(): return lax.ppermute(array, axis, pairs)]
    unnamed x11 -> x24, local copies, waits for them, and re-layouts: 15.2 us -> 27.5 us
    pallas_call x2 -> x5, Pallas kernels: 77.3 us -> 88.8 us  [the longest x1 31 us: top_gram_call(): pl.pallas_call(top_gram_kernel, out_shape=jax.ShapeDtypeStruct((RANK, 128...]
    pallas_call x1, Pallas kernels: 16.7 us -> 8.6 us  [gram_call(): pl.pallas_call(gram_kernel, out_shape=(jax.ShapeDtypeStruct((128 * RANK,...]
    pallas_call x1, Pallas kernels: 15.4 us -> 8.19 us  [apply_call(): pl.pallas_call(apply_kernel, out_shape=(jax.ShapeDtypeStruct(v.shape, F32...]
    ppermute x0 -> x8, starting transfers between devices: none -> 7.17 us  [the longest x6 6 us: turned_column(): return lax.ppermute(array, 'leaf', pairs)]
  transfers between devices with their start and end apart: 4 -> 11, of which waited for: 4 -> 2; matrix products, arithmetic and copies ran while one was open for 32% -> 14% of each run, Pallas kernels for 17% -> 35%
where the time goes in v2:
time: 219 us; the launch traced here: 216 us
  Pallas kernels  106 us (48%)
  waiting for transfers between devices  35.2 us (16%)
  local copies, waits for them, and re-layouts  31.5 us (14%)
  other arithmetic  15.1 us (7%)
  starting transfers between devices  14.6 us (7%)
  between operations  14.1 us (6%)
    pallas_call x1, Pallas kernels, top_gram_call(): pl.pallas_call(top_gram_kernel, out_shape=jax.ShapeDtypeStruct((RANK, 128...  31 us
    all_gather x1, waiting for transfers between devices, on_device(): frontier = lax.all_gather(carried, 'leaf', axis=0, tiled=False)  31 us
    unnamed x24, local copies, waits for them, and re-layouts  27.5 us
    pallas_call x1, Pallas kernels, right_call(): pl.pallas_call(right_kernel, grid_spec=pltpu.PrefetchScalarGridSpec(num_s...  22.2 us
    pallas_call x1, Pallas kernels, factor_call(): pl.pallas_call(factor_kernel, out_shape=(jax.ShapeDtypeStruct((RANK, 128,...  17.4 us
    pallas_call x1, other arithmetic, top_out_call(): pl.pallas_call(top_out_kernel, in_specs=[pl.BlockSpec(memory_space=pltpu....  15 us
    pallas_call x1, Pallas kernels, left_call(): pl.pallas_call(left_kernel, grid=(ROW // ROWS_STEP,), in_specs=[pl.BlockS...  13.7 us
    pallas_call x1, Pallas kernels, gram_call(): pl.pallas_call(gram_kernel, out_shape=(jax.ShapeDtypeStruct((128 * RANK,...  8.6 us
  transfers between devices with their start and end apart: 11, of which 2 were waited for; matrix products, arithmetic and copies ran while one was open for 14% of the time, Pallas kernels for 35%

profile of v2, /device:TPU:7, one launch (start us, length us, event | category | flops | bytes accessed | tf_op | source)
XLA Modules:
  0.0 216.1 jit_solution(3349506771097610993)
XLA Ops:
  7.2 0.0 all-gather.3.cloned.1.call-start
  7.2 0.0 copy-start.1
  7.2 1.6 copy-done.1
  8.8 0.0 copy-start.2
  8.8 1.6 copy-done.2
  10.4 8.6 %gram_up.1 = (f32[8192,128]{1,0:T(8,128)}, f32[32,128]{1,0:T(8,128)}) custom-call(f32[32,64,256]{2,1,0:T(8,128)S(1)} %copy-done.1, f32[63,64,64]{2,1,0:T(8,128)S(1)} %copy-done.2), custom_call_target="tpu_custom_call" | custom-call | flops 12000000 | bytes 30000000 | tf_op jit(solution)/shard_map/gram_up/pallas_call | solution.py:144
  19.0 0.0 all-gather.3.cloned.1.call-update
  19.0 17.4 %factor_local.1 = (f32[64,128,128]{2,1,0:T(8,128)S(1)}, f32[960,128]{1,0:T(8,128)S(1)}) custom-call(f32[8192,128]{1,0:T(8,128)} %get-tuple-element.43.g_ref), custom_call_target="tpu_custom_call" | custom-call | flops 15000000 | bytes 37500000 | tf_op jit(solution)/shard_map/factor_local/pallas_call | solution.py:176
  36.4 0.0 copy-start.4
  36.4 2.0 copy-done.4
  38.4 3.8 %collective-permute-start.4 = (f32[15,64,128]{2,1,0:T(8,128)S(1)}, f32[15,64,128]{2,1,0:T(8,128)S(1)}, u32[]{:S(2)}, u32[]{:S(2)}) collective-permute-start(f32[15,64,128]{2,1,0:T(8,128)S(1)} %bitcast.11), channel_id=1, source_target_pairs={{0,6},{1,7},{2,0},{3,1},{4,2},{5,3},{6,4},{7,5},{8,14},{9,15},{10,... | collective-permute-start | bytes 1474568 | tf_op jit(solution)/shard_map/ppermute | solution.py:423
  42.2 0.0 collective-permute-start.3
  42.2 0.7 collective-permute-start.2
  42.9 2.4 %collective-permute-start.1 = (f32[15,64,128]{2,1,0:T(8,128)S(1)}, f32[15,64,128]{2,1,0:T(8,128)S(1)}, u32[]{:S(2)}, u32[]{:S(2)}) collective-permute-start(f32[15,64,128]{2,1,0:T(8,128)S(1)} %bitcast.14), channel_id=1, source_target_pairs={{8,0},{9,1},{10,2},{11,3},{12,4},{13,5},{14,6},{15,7},{16,8},{17,9... | collective-permute-start | bytes 1474568 | tf_op jit(solution)/shard_map/ppermute | solution.py:412
  45.3 4.9 %collective-permute-start = (f32[15,64,128]{2,1,0:T(8,128)S(1)}, f32[15,64,128]{2,1,0:T(8,128)S(1)}, u32[]{:S(2)}, u32[]{:S(2)}) collective-permute-start(f32[15,64,128]{2,1,0:T(8,128)S(1)} %bitcast.15), channel_id=1, source_target_pairs={{0,8},{1,9},{2,10},{3,11},{4,12},{5,13},{6,14},{7,15},{8,16},{9,17... | collective-permute-start | bytes 1474568 | tf_op jit(solution)/shard_map/ppermute | solution.py:412
  50.3 0.0 copy-start.3
  50.3 4.5 %turn_local.1 = f32[4096,128]{1,0:T(8,128)S(1)} custom-call(f32[64,128,128]{2,1,0:T(8,128)} %copy-done.4), custom_call_target="tpu_custom_call" | custom-call | flops 6000000 | bytes 15000000 | tf_op jit(solution)/shard_map/turn_local/pallas_call | solution.py:193
  54.8 0.0 copy-done.3
  54.8 8.2 %apply_local.1 = (f32[32,64,256]{2,1,0:T(8,128)}, f32[63,64,64]{2,1,0:T(8,128)}) custom-call(f32[64,64,128]{2,1,0:T(8,128)S(1)} %bitcast.8, f32[32,64,256]{2,1,0:T(8,128)} %v_ref.3, f32[63,64,64]{2,1,0:T(8,128)S(1)} %copy-done.3), custom_call_target="tpu_custom_call" | custom-call | flops 9000000 | bytes 22500000 | tf_op jit(solution)/shard_map/apply_local/pallas_call | solution.py:225
  63.0 0.0 collective-permute-done.4
  63.0 0.0 collective-permute-done.3
  63.0 4.2 %collective-permute-done.2 = f32[15,64,128]{2,1,0:T(8,128)S(1)} collective-permute-done((f32[15,64,128]{2,1,0:T(8,128)S(1)}, f32[15,64,128]{2,1,0:T(8,128)S(1)}, u32[]{:S(2)}, u32[]{:S(2)}) %collective-permute-start.2) | collective-permute-done | bytes 491552 | tf_op jit(solution)/shard_map/ppermute | solution.py:423
  67.2 0.0 collective-permute-done.1
  67.2 0.0 collective-permute-done
  67.2 0.9 constant_dynamic-update-slice_fusion.3
  68.1 0.8 constant_dynamic-update-slice_fusion.2
  68.9 0.8 constant_dynamic-update-slice_fusion.1
  69.7 0.9 constant_dynamic-update-slice_fusion.a_ref
  70.6 0.9 collective-permute-start.5
  71.6 0.8 collective-permute-start.8
  72.4 0.0 collective-permute-start.7
  72.4 0.8 collective-permute-start.6
  73.1 5.6 %copy.10.e_ref = f32[126,64,64]{2,1,0:T(8,128)} copy(f32[126,64,64]{0,2,1:T(8,128)} %param.9) | data formatting | bytes 4128768 | tf_op args[2]
  78.7 13.7 %couple_left.1.z_ref = bf16[56,8,64,128]{3,2,1,0:T(8,128)(2,1)} custom-call(f32[56,8,64,64]{3,2,1,0:T(8,128)} %s_ref.1, f32[64,64,128]{2,1,0:T(8,128)S(1)} %bitcast.9), custom_call_target="tpu_custom_call" | custom-call | flops 17000000 | bytes 42500000 | tf_op jit(solution)/shard_map/couple_left/pallas_call | solution.py:327
  92.5 0.0 collective-permute-done.5.b_ref
  92.5 31.0 %all-gather.3.cloned.1.call-done = f32[4096,128]{1,0:T(8,128)} async-done(((f32[32,128]{1,0:T(8,128)}), f32[4096,128]{1,0:T(8,128)}) %all-gather.3.cloned.1.call-update) | async-done | bytes 2097168 | tf_op jit(solution)/shard_map/all_gather | solution.py:442
  123.4 0.0 copy-start
  123.4 2.2 %copy-done = f32[126,64,64]{2,1,0:T(8,128)S(1)} copy-done((f32[126,64,64]{2,1,0:T(8,128)S(1)}, f32[126,64,64]{2,1,0:T(8,128)}, u32[]{:S(2)}) %copy-start) | copy-done | bytes 2064408
  125.6 0.0 copy-start.5
  125.6 1.6 copy-done.5
  127.2 31.0 %top_gram.1 = f32[64,128,128]{2,1,0:T(8,128)} custom-call(f32[128,32,128]{2,1,0:T(8,128)S(1)} %bitcast.10, f32[126,64,64]{2,1,0:T(8,128)S(1)} %copy-done), custom_call_target="tpu_custom_call" | custom-call | flops 25000000 | bytes 62500000 | tf_op jit(solution)/shard_map/top_gram/pallas_call | solution.py:266
  158.2 0.0 collective-permute-done.8
  158.2 0.0 collective-permute-done.7
  158.2 0.0 collective-permute-done.6
  158.2 1.0 constant_dynamic-update-slice_fusion.9
  159.2 2.3 %constant_dynamic-update-slice_fusion.8 = f32[120,64,128]{2,1,0:T(8,128)} fusion(f32[120,64,128]{2,1,0:T(8,128)} %constant_dynamic-update-slice_fusion.9, f32[30,64,128]{2,1,0:T(8,128)} %collective-permute-done.6), kind=kLoop, calls=%fused_computation.39 | loop fusion | bytes 1966080
  161.5 0.0 copy-start.6
  161.5 2.3 %constant_dynamic-update-slice_fusion.7 = f32[120,64,128]{2,1,0:T(8,128)} fusion(f32[120,64,128]{2,1,0:T(8,128)} %constant_dynamic-update-slice_fusion.8, f32[30,64,128]{2,1,0:T(8,128)} %collective-permute-done.7), kind=kLoop, calls=%fused_computation.38 | loop fusion | bytes 1966080
  163.8 2.3 %constant_dynamic-update-slice_fusion.6.c_ref = f32[120,64,128]{2,1,0:T(8,128)} fusion(f32[120,64,128]{2,1,0:T(8,128)} %constant_dynamic-update-slice_fusion.7, f32[30,64,128]{2,1,0:T(8,128)} %collective-permute-done.8), kind=kLoop, calls=%fused_computation.37 | loop fusion | bytes 1966080 | tf_op jit(solution)/shard_map/concatenate | solution.py:461
  166.1 0.2 collective-permute-start.9
  166.3 0.0 copy-done.6
  166.3 0.1 copy.12
  166.4 0.1 fusion.5.where_ref
  166.5 0.8 slice_bitcast_fusion
  167.2 15.0 %top_out.1 = (f32[63,64,64]{2,1,0:T(8,128)}, f32[126,64,64]{2,1,0:T(8,128)}, f32[64,64]{1,0:T(8,128)}) fusion(f32[63,64,64]{2,1,0:T(8,128)} %get-tuple-element.48, s32[1]{0:T(128)} %bitcast.2, f32[64,128,128]{2,1,0:T(8,128)} %top_gram.1, f32[126,64,64]{2,1,0:T(8,128)} %copy.10.e_ref, f32[64,64]{1,0:T(8,128)S(1)} %slice_bitcast_fusion), kind=kCustom, calls=%fused_computation.17 | custom fusion | flops 17000000 | bytes 12534272 | tf_op jit(solution)/shard_map/top_out/pallas_call | solution.py:297
  182.2 4.8 %copy.15 = f32[126,64,64]{0,2,1:T(8,128)} copy(f32[126,64,64]{2,1,0:T(8,128)} %get-tuple-element.77) | data formatting | bytes 4128768
  187.1 0.0 collective-permute-done.9.d_ref
  187.1 22.2 %couple_right.1 = f32[56,8,64,64]{3,2,1,0:T(8,128)} custom-call(s32[56,8]{1,0:T(8,128)S(1)} %fusion.5.where_ref, bf16[56,8,64,128]{3,2,1,0:T(8,128)(2,1)} %couple_left.1.z_ref, f32[60,64,128]{2,1,0:T(8,128)} %constant_dynamic-update-slice_fusion.a_ref, f32[60,64,128]{2,1,0:T(8,128)} %collective-permute-done.5.b_ref, ...), custom_call_target="tpu_custom_call" | custom-call | flops 20000000 | bytes 50000000 | tf_op jit(solution)/shard_map/couple_right/pallas_call | solution.py:387
  (2 shorter events, 0.1 us)
Async XLA Ops:
  7.2 116.3 %all-gather.3.cloned.1.call-start = ((), (), s32[]{:S(2)}) async-start(), calls=%async_computation | async-start | bytes 2113536 | tf_op jit(solution)/shard_map/all_gather | solution.py:442
  7.2 1.6 copy-start.1
  8.8 1.6 copy-start.2
  36.4 2.0 copy-start.4
  38.4 24.6 %collective-permute-start.4 = (f32[15,64,128]{2,1,0:T(8,128)S(1)}, f32[15,64,128]{2,1,0:T(8,128)S(1)}, u32[]{:S(2)}, u32[]{:S(2)}) collective-permute-start(f32[15,64,128]{2,1,0:T(8,128)S(1)} %bitcast.11), channel_id=1, source_target_pairs={{0,6},{1,7},{2,0},{3,1},{4,2},{5,3},{6,4},{7,5},{8,14},{9,15},{10,... | collective-permute-start | bytes 1474568 | tf_op jit(solution)/shard_map/ppermute | solution.py:423
  42.2 20.8 %collective-permute-start.3 = (f32[15,64,128]{2,1,0:T(8,128)S(1)}, f32[15,64,128]{2,1,0:T(8,128)S(1)}, u32[]{:S(2)}, u32[]{:S(2)}) collective-permute-start(f32[15,64,128]{2,1,0:T(8,128)S(1)} %bitcast.12), channel_id=1, source_target_pairs={{0,4},{1,5},{2,6},{3,7},{4,0},{5,1},{6,2},{7,3},{8,12},{9,13},{10,... | collective-permute-start | bytes 1474568 | tf_op jit(solution)/shard_map/ppermute | solution.py:423
  42.2 25.0 %collective-permute-start.2 = (f32[15,64,128]{2,1,0:T(8,128)S(1)}, f32[15,64,128]{2,1,0:T(8,128)S(1)}, u32[]{:S(2)}, u32[]{:S(2)}) collective-permute-start(f32[15,64,128]{2,1,0:T(8,128)S(1)} %bitcast.13), channel_id=1, source_target_pairs={{0,2},{1,3},{2,4},{3,5},{4,6},{5,7},{6,0},{7,1},{8,10},{9,11},{10,... | collective-permute-start | bytes 1474568 | tf_op jit(solution)/shard_map/ppermute | solution.py:423
  42.9 24.3 %collective-permute-start.1 = (f32[15,64,128]{2,1,0:T(8,128)S(1)}, f32[15,64,128]{2,1,0:T(8,128)S(1)}, u32[]{:S(2)}, u32[]{:S(2)}) collective-permute-start(f32[15,64,128]{2,1,0:T(8,128)S(1)} %bitcast.14), channel_id=1, source_target_pairs={{8,0},{9,1},{10,2},{11,3},{12,4},{13,5},{14,6},{15,7},{16,8},{17,9... | collective-permute-start | bytes 1474568 | tf_op jit(solution)/shard_map/ppermute | solution.py:412
  45.3 21.9 %collective-permute-start = (f32[15,64,128]{2,1,0:T(8,128)S(1)}, f32[15,64,128]{2,1,0:T(8,128)S(1)}, u32[]{:S(2)}, u32[]{:S(2)}) collective-permute-start(f32[15,64,128]{2,1,0:T(8,128)S(1)} %bitcast.15), channel_id=1, source_target_pairs={{0,8},{1,9},{2,10},{3,11},{4,12},{5,13},{6,14},{7,15},{8,16},{9,17... | collective-permute-start | bytes 1474568 | tf_op jit(solution)/shard_map/ppermute | solution.py:412
  50.3 4.5 %copy-start.3 = (f32[63,64,64]{2,1,0:T(8,128)S(1)}, f32[63,64,64]{2,1,0:T(8,128)}, u32[]{:S(2)}) copy-start(f32[63,64,64]{2,1,0:T(8,128)} %e_ref.5) | copy-start | bytes 3096580
  70.6 21.9 %collective-permute-start.5 = (f32[60,64,128]{2,1,0:T(8,128)}, f32[60,64,128]{2,1,0:T(8,128)}, u32[]{:S(2)}, u32[]{:S(2)}) collective-permute-start(f32[60,64,128]{2,1,0:T(8,128)} %constant_dynamic-update-slice_fusion.a_ref), channel_id=1, source_target_pairs={{0,1},{1,0},{2,3},{3,2},{4,5},{5,4},{6,7},{7,6},{8,9},{9,8},{10,11... | collective-permute-start | bytes 5898248 | tf_op jit(solution)/shard_map/ppermute | solution.py:417
  71.6 86.6 %collective-permute-start.8 = (f32[30,64,128]{2,1,0:T(8,128)S(1)}, f32[30,64,128]{2,1,0:T(8,128)}, u32[]{:S(2)}, u32[]{:S(2)}) collective-permute-start(f32[30,64,128]{2,1,0:T(8,128)S(1)} %constant_dynamic-update-slice_fusion.4), channel_id=1, source_target_pairs={{0,6},{1,7},{2,0},{3,1},{4,2},{5,3},{6,4},{7,5},{8,14},{9,15},{10,... | collective-permute-start | bytes 2949128 | tf_op jit(solution)/shard_map/ppermute | solution.py:423
  72.4 85.9 %collective-permute-start.7 = (f32[30,64,128]{2,1,0:T(8,128)S(1)}, f32[30,64,128]{2,1,0:T(8,128)}, u32[]{:S(2)}, u32[]{:S(2)}) collective-permute-start(f32[30,64,128]{2,1,0:T(8,128)S(1)} %constant_dynamic-update-slice_fusion.4), channel_id=1, source_target_pairs={{0,4},{1,5},{2,6},{3,7},{4,0},{5,1},{6,2},{7,3},{8,12},{9,13},{10,... | collective-permute-start | bytes 2949128 | tf_op jit(solution)/shard_map/ppermute | solution.py:423
  72.4 85.9 %collective-permute-start.6 = (f32[30,64,128]{2,1,0:T(8,128)S(1)}, f32[30,64,128]{2,1,0:T(8,128)}, u32[]{:S(2)}, u32[]{:S(2)}) collective-permute-start(f32[30,64,128]{2,1,0:T(8,128)S(1)} %constant_dynamic-update-slice_fusion.4), channel_id=1, source_target_pairs={{0,2},{1,3},{2,4},{3,5},{4,6},{5,7},{6,0},{7,1},{8,10},{9,11},{10,... | collective-permute-start | bytes 2949128 | tf_op jit(solution)/shard_map/ppermute | solution.py:423
  123.4 2.2 %copy-start = (f32[126,64,64]{2,1,0:T(8,128)S(1)}, f32[126,64,64]{2,1,0:T(8,128)}, u32[]{:S(2)}) copy-start(f32[126,64,64]{2,1,0:T(8,128)} %copy.10.e_ref) | copy-start | bytes 6193156
  125.6 1.6 copy-start.5
  161.5 4.8 %copy-start.6 = (s32[56,8]{0,1:T(8,128)S(1)}, s32[56,8]{0,1:T(8,128)}, u32[]{:S(2)}) copy-start(s32[56,8]{0,1:T(8,128)} %param.11) | copy-start | bytes 5380
  166.1 21.0 %collective-permute-start.9 = (f32[120,64,128]{2,1,0:T(8,128)}, f32[120,64,128]{2,1,0:T(8,128)}, u32[]{:S(2)}, u32[]{:S(2)}) collective-permute-start(f32[120,64,128]{2,1,0:T(8,128)} %constant_dynamic-update-slice_fusion.6.c_ref), channel_id=1, source_target_pairs={{0,1},{1,0},{2,3},{3,2},{4,5},{5,4},{6,7},{7,6},{8,9},{9,8},{10,11... | collective-permute-start | bytes 11796488 | tf_op jit(solution)/shard_map/ppermute | solution.py:417
Sparse Core Ops, SparseCore 0:
  19.1 104.2 all-gather.2

commit v3 on v2

--- a/solution.py
+++ b/solution.py
@@ -17,7 +17,9 @@
 COLUMN = 8
 TOPN = 127
 ROWS_STEP = 8
-VMEM_LIMIT = 48 * 1024 * 1024
+UNROLL = 4
+CHUNKS = 4
+MIB = 1024 * 1024
 F32 = jnp.float32
 BF16 = jnp.bfloat16
 FULL = lax.Precision.HIGHEST
@@ -51,8 +53,8 @@
     return pl.CostEstimate(flops=us * 1_000_000, bytes_accessed=us * 2_500_000, transcendentals=0)
 
 
-def params():
-    return pltpu.CompilerParams(vmem_limit_bytes=VMEM_LIMIT)
+def params(mib):
+    return pltpu.CompilerParams(vmem_limit_bytes=mib * MIB)
 
 
 def load_lanes(g_ref, w_ref):
@@ -110,13 +112,27 @@
     return pl.ds(pl.multiple_of(n * RANK, RANK), RANK)
 
 
-def gram_kernel(v_ref, e_ref, g_ref, c_ref):
+def gram_kernel(v_hbm, e_hbm, g_ref, c_ref, v_ref, e_ref, sems):
+    chunk = LEAF // CHUNKS
+    copies = [
+        pltpu.make_async_copy(
+            v_hbm.at[pl.ds(k * chunk, chunk)], v_ref.at[pl.ds(k * chunk, chunk)], sems.at[k]
+        )
+        for k in range(CHUNKS)
+    ]
+    copies.append(pltpu.make_async_copy(e_hbm, e_ref, sems.at[CHUNKS]))
+    for copy in copies:
+        copy.start()
+
     def leaf(b, carry):
         v = v_ref[b]
         g_ref[block_at(b), 0:RANK] = exact(v, v, NT)
         return carry
 
-    lax.fori_loop(0, LEAF, leaf, 0, unroll=8)
+    for k in range(CHUNKS):
+        copies[k].wait()
+        lax.fori_loop(k * chunk, (k + 1) * chunk, leaf, 0, unroll=chunk)
+    copies[CHUNKS].wait()
 
     def parent(p, carry):
         a = 2 * (p - LEAF)
@@ -147,13 +163,19 @@
             jax.ShapeDtypeStruct((128 * RANK, 128), F32),
             jax.ShapeDtypeStruct((32, 128), F32),
         ),
-        compiler_params=params(),
+        in_specs=[pl.BlockSpec(memory_space=pl.ANY)] * 2,
+        scratch_shapes=[
+            pltpu.VMEM(v.shape, F32),
+            pltpu.VMEM(e.shape, F32),
+            pltpu.SemaphoreType.DMA((CHUNKS + 1,)),
+        ],
+        compiler_params=params(62),
         cost_estimate=cost(12),
         name="gram_up",
     )(v, e)
 
 
-def factor_kernel(g_ref, w_ref, unit_ref):
+def factor_kernel(g_ref, um_ref, unit_ref, w_ref):
     load_lanes(g_ref, w_ref)
     eliminate(w_ref)
     place = lax.broadcasted_iota(jnp.int32, (RANK, 128), 0)
@@ -170,36 +192,24 @@
 
     diag = lax.fori_loop(0, RANK, pack, jnp.zeros((RANK, 128), F32), unroll=8)
     unit_ref[QUART * RANK :, :] = jnp.concatenate([diag, diag], axis=0).T[0:RANK]
+    store_lanes(w_ref, um_ref, RANK)
 
 
 def factor_call(g):
     return pl.pallas_call(
         factor_kernel,
         out_shape=(
-            jax.ShapeDtypeStruct((RANK, 128, 128), F32),
+            jax.ShapeDtypeStruct((RANK * RANK, 128), F32),
             jax.ShapeDtypeStruct((UNIT * RANK, 128), F32),
         ),
-        compiler_params=params(),
+        scratch_shapes=[pltpu.VMEM((RANK, 128, 128), F32)],
+        compiler_params=params(48),
         cost_estimate=cost(15),
         name="factor_local",
     )(g)
 
 
-def turn_kernel(w_ref, um_ref):
-    store_lanes(w_ref, um_ref, RANK)
-
-
-def turn_call(w):
-    return pl.pallas_call(
-        turn_kernel,
-        out_shape=jax.ShapeDtypeStruct((RANK * RANK, 128), F32),
-        compiler_params=params(),
-        cost_estimate=cost(6),
-        name="turn_local",
-    )(w)
-
-
-def apply_kernel(um_ref, v_ref, e_ref, leaves_ref, moved_ref):
+def apply_kernel(um_ref, v_ref, e_ref, top_ref, leaves_ref, moved_ref):
     def leaf(b, carry):
         m = um_ref[b, :, RANK:128]
         leaves_ref[b] = mul3(m, v_ref[b], NN)
@@ -221,26 +231,25 @@
     moved_ref[NODES - 1] = mul3(um_ref[NODES - 1, :, 0:RANK], e_ref[NODES - 1], NN)
 
 
-def apply_call(um, v, e):
+def apply_call(um, v, e, top):
+    vm = pl.BlockSpec(memory_space=pltpu.VMEM)
     return pl.pallas_call(
         apply_kernel,
+        in_specs=[vm, vm, vm, pl.BlockSpec(memory_space=pl.ANY)],
         out_shape=(
             jax.ShapeDtypeStruct(v.shape, F32),
             jax.ShapeDtypeStruct(e.shape, F32),
         ),
-        compiler_params=params(),
+        compiler_params=params(48),
         cost_estimate=cost(9),
         name="apply_local",
-    )(um, v, e)
-
-
-def top_gram_kernel(c_ref, e_ref, w_ref, g_ref):
-    def wide(d):
-        x = c_ref[d]
-        return jnp.concatenate([x[:, 0:RANK], x[:, RANK:128]], axis=0)
-
+    )(um, v, e, top)
+
+
+def top_kernel(own_ref, c_ref, e_ref, p_ref, new_ref, root_ref, mine_ref, g_ref, w_ref, um_ref):
     def first(p, carry):
-        g_ref[block_at(63 + p), 0:RANK] = wide(2 * p) + wide(2 * p + 1)
+        x = c_ref[p]
+        g_ref[block_at(63 + p), 0:RANK] = jnp.concatenate([x[:, 0:RANK], x[:, RANK:128]], axis=0)
         return carry
 
     lax.fori_loop(0, 64, first, 0, unroll=16)
@@ -260,20 +269,6 @@
     g_ref[TOPN * RANK :, :] = jnp.zeros_like(g_ref[TOPN * RANK :, :])
     load_lanes(g_ref, w_ref)
     eliminate(w_ref)
-
-
-def top_gram_call(c, e):
-    return pl.pallas_call(
-        top_gram_kernel,
-        out_shape=jax.ShapeDtypeStruct((RANK, 128, 128), F32),
-        scratch_shapes=[pltpu.VMEM((128 * RANK, 128), F32)],
-        compiler_params=params(),
-        cost_estimate=cost(25),
-        name="top_gram",
-    )(c, e)
-
-
-def top_out_kernel(own_ref, w_ref, e_ref, p_ref, new_ref, root_ref, mine_ref, um_ref):
     store_lanes(w_ref, um_ref, 128)
 
     def out(n, carry):
@@ -288,63 +283,39 @@
 
     lax.fori_loop(0, 63, out, 0, unroll=9)
     root_ref[...] = um_ref[0:RANK, 0:RANK]
-    up = 63 + own_ref[0] // 2
-    mine_ref[...] = mul3(p_ref[...], um_ref[block_at(up), RANK:128], NT)
-
-
-def top_out_call(own, w, e, p):
+    up = um_ref[block_at(63 + own_ref[0] // 2), RANK:128]
+    mine_ref[...] = mul3(p_ref[...], up, NT)
+
+
+def top_call(own, c, e, p):
     vm = pl.BlockSpec(memory_space=pltpu.VMEM)
     return pl.pallas_call(
-        top_out_kernel,
+        top_kernel,
         in_specs=[pl.BlockSpec(memory_space=pltpu.SMEM), vm, vm, vm],
         out_shape=(
             jax.ShapeDtypeStruct(e.shape, F32),
             jax.ShapeDtypeStruct((RANK, RANK), F32),
             jax.ShapeDtypeStruct((RANK, RANK), F32),
         ),
-        scratch_shapes=[pltpu.VMEM((128 * RANK, 128), F32)],
-        compiler_params=params(),
-        cost_estimate=cost(17),
-        name="top_out",
-    )(own, w, e, p)
-
-
-def left_kernel(s_ref, um_ref, z_ref):
-    first = pl.program_id(0) * ROWS_STEP
-
-    def one(r, carry):
-        u = split(um_ref[first + r, :, 0:RANK])
-        for c in range(CPL):
-            z = three(u, split(s_ref[r, c]), NN)
-            high = z.astype(BF16).astype(F32)
-            z_ref[r, c] = jnp.concatenate([high, z - high], axis=1).astype(BF16)
-        return carry
-
-    lax.fori_loop(0, ROWS_STEP, one, 0, unroll=4)
-
-
-def left_call(s, um):
-    return pl.pallas_call(
-        left_kernel,
-        grid=(ROW // ROWS_STEP,),
-        in_specs=[
-            pl.BlockSpec((ROWS_STEP, CPL, RANK, RANK), lambda r: (r, 0, 0, 0)),
-            pl.BlockSpec(memory_space=pltpu.VMEM),
+        scratch_shapes=[
+            pltpu.VMEM((128 * RANK, 128), F32),
+            pltpu.VMEM((RANK, 128, 128), F32),
+            pltpu.VMEM((128 * RANK, 128), F32),
         ],
-        out_specs=pl.BlockSpec((ROWS_STEP, CPL, RANK, 128), lambda r: (r, 0, 0, 0)),
-        out_shape=jax.ShapeDtypeStruct((ROW, CPL, RANK, 128), BF16),
-        compiler_params=params(),
-        cost_estimate=cost(17),
-        name="couple_left",
-    )(s, um)
-
-
-def right_kernel(where_ref, z_ref, a_ref, b_ref, c_ref, d_ref, out_ref, win_ref, sems):
+        compiler_params=params(48),
+        cost_estimate=cost(42),
+        name="top_tree",
+    )(own, c, e, p)
+
+
+def couple_kernel(where_ref, s_ref, um_ref, *refs):
+    *piece_refs, out_ref, win_ref, sems = refs
+
     @pl.when(pl.program_id(0) == 0)
     def _():
         copies = []
         begin = 0
-        for k, piece in enumerate((a_ref, b_ref, c_ref, d_ref)):
+        for k, piece in enumerate(piece_refs):
             amount = piece.shape[0]
             target = win_ref.at[pl.ds(begin, amount)]
             copies.append(pltpu.make_async_copy(piece, target, sems.at[k]))
@@ -359,8 +330,10 @@
     over = lax.broadcasted_iota(jnp.int32, (RANK, RANK), 1)
 
     def one(r, carry):
+        row = first + r
+        rights = []
         for c in range(CPL):
-            code = where_ref[first + r, c]
+            code = where_ref[row, c]
             unit = code // 64
             local = code % 64
             quarter = local // QUART
@@ -372,38 +345,37 @@
             strict = jnp.where(second, plain, turned)
             on = jnp.where(second, jnp.broadcast_to(diag, (RANK, RANK)), turned)
             lower = jnp.where(down > over, strict, jnp.where(down == over, on, 0.0))
-            high, low = split(lower)
-            z = z_ref[r, c]
-            dot = functools.partial(
-                lax.dot_general, dimension_numbers=NN, preferred_element_type=F32
-            )
-            out_ref[r, c] = dot(z, jnp.concatenate([high, high], axis=0)) + dot(z[:, 0:RANK], low)
-        return carry
-
-    lax.fori_loop(0, ROWS_STEP, one, 0, unroll=4)
-
-
-def right_call(where, z, pieces):
+            rights.append(mul3(s_ref[r, c], lower, NN))
+        u = split(um_ref[row, :, 0:RANK])
+        for c in range(CPL):
+            out_ref[r, c] = three(u, split(rights[c]), NN)
+        return carry
+
+    lax.fori_loop(0, ROWS_STEP, one, 0, unroll=UNROLL)
+
+
+def couple_call(where, s, um, pieces):
+    def block():
+        return pl.BlockSpec((ROWS_STEP, CPL, RANK, RANK), lambda r, w: (r, 0, 0, 0))
+
     return pl.pallas_call(
-        right_kernel,
+        couple_kernel,
         grid_spec=pltpu.PrefetchScalarGridSpec(
             num_scalar_prefetch=1,
             grid=(ROW // ROWS_STEP,),
-            in_specs=[
-                pl.BlockSpec((ROWS_STEP, CPL, RANK, 128), lambda r, w: (r, 0, 0, 0)),
-            ]
-            + [pl.BlockSpec(memory_space=pl.ANY)] * 4,
-            out_specs=pl.BlockSpec((ROWS_STEP, CPL, RANK, RANK), lambda r, w: (r, 0, 0, 0)),
+            in_specs=[block(), pl.BlockSpec(memory_space=pltpu.VMEM)]
+            + [pl.BlockSpec(memory_space=pl.ANY)] * len(pieces),
+            out_specs=block(),
             scratch_shapes=[
                 pltpu.VMEM((3 * COLUMN * UNIT, RANK, 128), F32),
-                pltpu.SemaphoreType.DMA((4,)),
+                pltpu.SemaphoreType.DMA((len(pieces),)),
             ],
         ),
         out_shape=jax.ShapeDtypeStruct((ROW, CPL, RANK, RANK), F32),
-        compiler_params=params(),
-        cost_estimate=cost(20),
-        name="couple_right",
-    )(where, z, *pieces)
+        compiler_params=params(28),
+        cost_estimate=cost(32),
+        name="couple",
+    )(where, s, um, *pieces)
 
 
 def shifted(array, axis, by):
@@ -434,37 +406,39 @@
     steps = (own % COLUMN // 2 - device_of % COLUMN // 2) % (COLUMN // 2)
     other = (device_of + own) % 2
     place = jnp.where(
-        side == 0, 4 * other + steps, 8 + 8 * other + 2 * steps + (side > 0).astype(jnp.int32)
-    )
+        side == 0, steps, 4 + 2 * steps + (side > 0).astype(jnp.int32)
+    ) + 12 * other
     where = place * 64 + coupling_cols % ROW
 
+    devices = lax.axis_size("leaf")
+    columns = devices // COLUMN
+    along = [[c * COLUMN + j for j in range(COLUMN)] for c in range(columns)]
+    across = [[c * COLUMN + j for c in range(columns)] for j in range(COLUMN)]
     grams, carried = gram_call(leaf_bases, transfers)
-    frontier = lax.all_gather(carried, "leaf", axis=0, tiled=False)
-    wide, unit = factor_call(grams)
+    joined = lax.all_gather(carried, "leaf", axis_index_groups=along, axis=0, tiled=False)
+    joined = joined[0::2] + joined[1::2]
+    joined, grams = together(joined, grams)
+    frontier = lax.all_gather(joined, "leaf", axis_index_groups=across, axis=0, tiled=True)
+
+    um, unit = factor_call(grams)
+    um = um.reshape(RANK, RANK, 128)
     unit = unit.reshape(UNIT, RANK, 128)
     before = shifted(unit, "leaf", COLUMN)
     after = shifted(unit, "leaf", -COLUMN)
     line = [unit] + [turned_column(unit, by) for by in (1, 2, 3)]
-    um = turn_call(wide).reshape(RANK, RANK, 128)
-    new_leaves, moved = apply_call(um, leaf_bases, transfers)
-    moved, um, before, after, *line = together(moved, um, before, after, *line)
-
-    near = jnp.concatenate(line, axis=0)
-    near_other = swapped(near)
+    new_leaves, moved = apply_call(um, leaf_bases, transfers, top_transfers)
     pair = jnp.concatenate([before, after], axis=0)
+    pair, moved, um, *line = together(pair, moved, um, *line)
     sides = [pair] + [turned_column(pair, by) for by in (1, 2, 3)]
-    left = left_call(couplings, um)
-    left, near_other, frontier = together(left, near_other, frontier)
-
-    top_wide = top_gram_call(frontier, top_transfers)
-    top_wide, left, *sides = together(top_wide, left, *sides)
-    far = jnp.concatenate(sides, axis=0)
-    far_other = swapped(far)
-    new_top, root_factor, mine = top_out_call(
-        own.reshape(1), top_wide, top_transfers, moved[NODES - 1]
+    new_top, root_factor, mine = top_call(
+        own.reshape(1), frontier, top_transfers, moved[NODES - 1]
     )
+    mine, *rest = together(mine, *line, *sides)
+    line, sides = rest[0:4], rest[4:8]
+    line_other = [swapped(part) for part in line]
+    sides_other = [swapped(part) for part in sides]
     new_transfers = moved.at[NODES - 1].set(mine)
-    new_couplings = right_call(where, left, (near, near_other, far, far_other))
+    new_couplings = couple_call(where, couplings, um, line + sides + line_other + sides_other)
     return (new_leaves, new_transfers, new_top, root_factor, new_couplings)
 
 

time: 219 us -> 188 us (0.86); the launches traced: 216 us -> 188 us
  waiting for transfers between devices: 35.2 us -> 6.63 us
  blocking collectives: 0 us -> 14.7 us
  other arithmetic: 15.1 us -> 2 us
  local copies, waits for them, and re-layouts: 31.5 us -> 22.1 us
  starting transfers between devices: 14.6 us -> 19.4 us
  Pallas kernels: 106 us -> 109 us
    all_gather x1, waiting for transfers between devices: 31 us -> 0.01 us  [on_device(): lax.all_gather(joined, 'leaf', axis_index_groups=across, axis=0, tiled=True)]
    pallas_call x1 -> x0, other arithmetic: 15 us -> none  [top_out_call(): pl.pallas_call(top_out_kernel, in_specs=[pl.BlockSpec(memory_space=pltpu....]
    all_gather x0 -> x1, blocking collectives: none -> 14.7 us  [on_device(): lax.all_gather(carried, 'leaf', axis_index_groups=along, axis=0, tiled=Fa...]
    unnamed x24 -> x23, local copies, waits for them, and re-layouts: 27.5 us -> 20.7 us
    concatenate x3 -> x0, local copies, waits for them, and re-layouts: 3.16 us -> none  [the longest x1 2.25 us: on_device(): far = jnp.concatenate(sides, axis=0)]
    ppermute x2 -> x8, starting transfers between devices: 1.17 us -> 3.85 us  [swapped(): return lax.ppermute(array, 'leaf', [(i, i ^ 1) for i in range(devices)])]
    pallas_call x6 -> x4, Pallas kernels: 97 us -> 99.2 us  [the longest x1 41 us: top_call(): pl.pallas_call(top_kernel, in_specs=[pl.BlockSpec(memory_space=pltpu.SMEM...]
  transfers between devices with their start and end apart: 11 -> 17, of which waited for: 2 -> 4; matrix products, arithmetic and copies ran while one was open for 14% -> 7% of each run, Pallas kernels for 35% -> 37%
where the time goes in v3:
time: 188 us
  Pallas kernels  109 us (58%)
  local copies, waits for them, and re-layouts  22.1 us (12%)
  starting transfers between devices  19.4 us (10%)
  blocking collectives  14.7 us (8%)
  between operations  14.1 us (8%)
  waiting for transfers between devices  6.63 us (4%)
  other arithmetic  2 us (1%)
    pallas_call x1, Pallas kernels, top_call(): pl.pallas_call(top_kernel, in_specs=[pl.BlockSpec(memory_space=pltpu.SMEM...  41 us
    pallas_call x1, Pallas kernels, couple_call(): pl.pallas_call(couple_kernel, grid_spec=pltpu.PrefetchScalarGridSpec(num_...  29.9 us
    unnamed x23, local copies, waits for them, and re-layouts  20.7 us
    pallas_call x1, Pallas kernels, factor_call(): pl.pallas_call(factor_kernel, out_shape=(jax.ShapeDtypeStruct((RANK * RAN...  20.1 us
    all_gather x1, blocking collectives, on_device(): lax.all_gather(carried, 'leaf', axis_index_groups=along, axis=0, tiled=Fa...  14.7 us
    pallas_call x1, Pallas kernels, gram_call(): pl.pallas_call(gram_kernel, out_shape=(jax.ShapeDtypeStruct((128 * RANK,...  9.68 us
    pallas_call x1, Pallas kernels, apply_call(): pl.pallas_call(apply_kernel, in_specs=[vm, vm, vm, pl.BlockSpec(memory_sp...  8.21 us
    ppermute x6, starting transfers between devices, turned_column(): return lax.ppermute(array, 'leaf', pairs)  8.11 us
  transfers between devices with their start and end apart: 17, of which 4 were waited for; matrix products, arithmetic and copies ran while one was open for 7% of the time, Pallas kernels for 37%

profile of v3, /device:TPU:7, one launch (start us, length us, event | category | flops | bytes accessed | tf_op | source)
XLA Modules:
  0.0 187.8 jit_solution(4944420139671634200)
XLA Ops:
  7.2 0.0 all-gather.3.cloned.1.call-start
  7.2 9.7 %gram_up.1 = (f32[8192,128]{1,0:T(8,128)}, f32[32,128]{1,0:T(8,128)}) custom-call(f32[32,64,256]{2,1,0:T(8,128)} %v_ref.1, f32[63,64,64]{2,1,0:T(8,128)} %e_ref.2), custom_call_target="tpu_custom_call" | custom-call | flops 12000000 | bytes 30000000 | tf_op jit(solution)/shard_map/gram_up/pallas_call | solution.py:160
  16.9 14.7 %all-gather = f32[256,128]{1,0:T(8,128)S(1)} all-gather(f32[32,128]{1,0:T(8,128)} %get-tuple-element.44), channel_id=2, replica_groups={{0,1,2,3,4,5,6,7},{8,9,10,11,12,13,14,15},{16,17,18,19,20,21,22,23},{24..., dimensions={0}, use_global_device_ids=true | all-gather | bytes 147456 | tf_op jit(solution)/shard_map/all_gather | solution.py:418
  31.6 0.6 slice_add_fusion
  32.2 0.0 all-gather.3.cloned.1.call-update
  32.2 20.1 %factor_local.1 = (f32[4096,128]{1,0:T(8,128)S(1)}, f32[960,128]{1,0:T(8,128)}) custom-call(f32[8192,128]{1,0:T(8,128)} %get-tuple-element.46.g_ref), custom_call_target="tpu_custom_call" | custom-call | flops 15000000 | bytes 37500000 | tf_op jit(solution)/shard_map/factor_local/pallas_call | solution.py:199
  52.3 2.4 %collective-permute-start.1 = (f32[15,64,128]{2,1,0:T(8,128)}, f32[15,64,128]{2,1,0:T(8,128)}, u32[]{:S(2)}, u32[]{:S(2)}) collective-permute-start(f32[15,64,128]{2,1,0:T(8,128)} %bitcast.2.refs_0_), channel_id=1, source_target_pairs={{8,0},{9,1},{10,2},{11,3},{12,4},{13,5},{14,6},{15,7},{16,8},{17,9... | collective-permute-start | bytes 1474568 | tf_op jit(solution)/shard_map/ppermute | solution.py:384
  54.7 4.9 %collective-permute-start = (f32[15,64,128]{2,1,0:T(8,128)}, f32[15,64,128]{2,1,0:T(8,128)}, u32[]{:S(2)}, u32[]{:S(2)}) collective-permute-start(f32[15,64,128]{2,1,0:T(8,128)} %bitcast.2.refs_0_), channel_id=1, source_target_pairs={{0,8},{1,9},{2,10},{3,11},{4,12},{5,13},{6,14},{7,15},{8,16},{9,17... | collective-permute-start | bytes 1474568 | tf_op jit(solution)/shard_map/ppermute | solution.py:384
  59.7 1.4 collective-permute-start.2
  61.1 2.4 %collective-permute-start.3 = (f32[15,64,128]{2,1,0:T(8,128)}, f32[15,64,128]{2,1,0:T(8,128)}, u32[]{:S(2)}, u32[]{:S(2)}) collective-permute-start(f32[15,64,128]{2,1,0:T(8,128)} %bitcast.2.refs_0_), channel_id=1, source_target_pairs={{0,4},{1,5},{2,6},{3,7},{4,0},{5,1},{6,2},{7,3},{8,12},{9,13},{10,... | collective-permute-start | bytes 1474568 | tf_op jit(solution)/shard_map/ppermute | solution.py:395
  63.5 0.1 collective-permute-start.4
  63.6 5.5 %copy.16.top_ref.e_ref = f32[126,64,64]{2,1,0:T(8,128)} copy(f32[126,64,64]{0,2,1:T(8,128)} %param.9) | data formatting | bytes 4128768 | tf_op args[2]
  69.1 0.0 copy-start
  69.1 1.6 copy-done
  70.7 8.2 %apply_local.1 = (f32[32,64,256]{2,1,0:T(8,128)}, f32[63,64,64]{2,1,0:T(8,128)}) custom-call(f32[64,64,128]{2,1,0:T(8,128)S(1)} %bitcast.8, f32[32,64,256]{2,1,0:T(8,128)} %v_ref.1, f32[63,64,64]{2,1,0:T(8,128)S(1)} %copy-done, f32[126,64,64]{2,1,0:T(8,128)} %copy.16.top_ref.e_ref), custom_call_target="tpu_custom_call" | custom-call | flops 9000000 | bytes 22500000 | tf_op jit(solution)/shard_map/apply_local/pallas_call | solution.py:236
  78.9 0.0 collective-permute-done.1
  78.9 0.0 collective-permute-done
  78.9 1.2 pad_maximum_fusion.refs_4_
  80.2 0.0 collective-permute-done.2.refs_1_
  80.2 4.7 %collective-permute-done.3.refs_2_ = f32[15,64,128]{2,1,0:T(8,128)} collective-permute-done((f32[15,64,128]{2,1,0:T(8,128)}, f32[15,64,128]{2,1,0:T(8,128)}, u32[]{:S(2)}, u32[]{:S(2)}) %collective-permute-start.3) | collective-permute-done | bytes 491552 | tf_op jit(solution)/shard_map/ppermute | solution.py:395
  84.9 0.0 collective-permute-done.4.refs_3_
  84.9 1.8 collective-permute-start.5
  86.7 2.4 %collective-permute-start.6 = (f32[30,64,128]{2,1,0:T(8,128)S(1)}, f32[30,64,128]{2,1,0:T(8,128)}, u32[]{:S(2)}, u32[]{:S(2)}) collective-permute-start(f32[30,64,128]{2,1,0:T(8,128)S(1)} %pad_maximum_fusion.refs_4_), channel_id=1, source_target_pairs={{0,4},{1,5},{2,6},{3,7},{4,0},{5,1},{6,2},{7,3},{8,12},{9,13},{10,... | collective-permute-start | bytes 2949128 | tf_op jit(solution)/shard_map/ppermute | solution.py:395
  89.1 0.0 collective-permute-start.7
  89.1 0.8 slice_bitcast_fusion.p_ref
  89.9 0.0 copy-start.2
  89.9 1.2 copy-done.2
  91.1 0.0 copy-start.9
  91.1 41.0 %top_tree.1 = (f32[126,64,64]{2,1,0:T(8,128)S(1)}, f32[64,64]{1,0:T(8,128)}, f32[64,64]{1,0:T(8,128)S(1)}) custom-call(s32[1]{0:T(128)} %bitcast.3.own_ref, f32[64,32,128]{2,1,0:T(8,128)S(1)} %copy-done.2, f32[126,64,64]{2,1,0:T(8,128)} %copy.16.top_ref.e_ref, f32[64,64]{1,0:T(8,128)S(1)} %slice_bitcast_fusion.p_ref), custom_call_target="tpu_custom_call" | custom-call | flops 42000000 | bytes 105000000 | tf_op jit(solution)/shard_map/top_tree/pallas_call | solution.py:292
  132.1 0.0 copy-start.1
  132.1 2.0 %copy-done.1 = f32[126,64,64]{2,1,0:T(8,128)} copy-done((f32[126,64,64]{2,1,0:T(8,128)}, f32[126,64,64]{2,1,0:T(8,128)S(1)}, u32[]{:S(2)}) %copy-start.1) | copy-done | bytes 2064408
  134.1 0.0 collective-permute-done.5.refs_5_
  134.1 0.0 collective-permute-done.6.refs_6_
  134.1 0.0 collective-permute-done.7.refs_7_
  134.1 1.7 collective-permute-start.8
  135.8 0.1 collective-permute-start.9
  135.9 0.4 collective-permute-start.10
  136.3 0.1 collective-permute-start.12
  136.4 0.4 collective-permute-start.13
  136.9 0.7 collective-permute-done.8.refs_8_
  137.5 0.8 copy-done.3
  138.3 0.4 collective-permute-start.14
  138.7 0.3 collective-permute-done.9.refs_9_
  138.9 0.0 copy-start.5
  138.9 0.8 copy-done.5
  139.8 0.4 collective-permute-start.15
  140.1 0.9 collective-permute-done.10.refs_10_
  141.0 0.8 copy-done.7
  141.8 0.4 collective-permute-start.11
  142.2 0.0 copy-done.9
  142.2 0.1 copy.18
  142.3 0.1 fusion.8.where_ref
  142.4 4.8 %copy.21 = f32[126,64,64]{0,2,1:T(8,128)} copy(f32[126,64,64]{2,1,0:T(8,128)} %copy-done.1) | data formatting | bytes 4128768
  147.2 0.6 bitcast_dynamic-update-slice_fusion
  147.9 0.0 collective-permute-done.11.refs_11_
  147.9 0.0 collective-permute-done.12.refs_12_
  147.9 0.0 collective-permute-done.13.refs_13_
  147.9 0.0 collective-permute-done.14.refs_14_
  147.9 0.0 collective-permute-done.15.refs_15_
  147.9 0.0 copy-start.4
  147.9 1.0 copy-done.4
  148.9 1.0 copy-done.6
  150.0 1.0 copy-done.8
  151.0 29.9 %couple.1 = f32[56,8,64,64]{3,2,1,0:T(8,128)} custom-call(s32[56,8]{1,0:T(8,128)S(1)} %fusion.8.where_ref, f32[56,8,64,64]{3,2,1,0:T(8,128)} %s_ref.1, f32[64,64,128]{2,1,0:T(8,128)S(1)} %bitcast.9, f32[15,64,128]{2,1,0:T(8,128)} %bitcast.2.refs_0_, f32[15,64,128]{2,1,0:T(8,128)} %collective-permute-done.2.refs_1_, ...), custom_call_target="tpu_custom_call" | custom-call | flops 32000000 | bytes 80000000 | tf_op jit(solution)/shard_map/couple/pallas_call | solution.py:361
  (5 shorter events, 0.0 us)
Async XLA Ops:
  7.2 82.7 %all-gather.3.cloned.1.call-start = ((), (), s32[]{:S(2)}) async-start(), calls=%async_computation | async-start | bytes 1114112 | tf_op jit(solution)/shard_map/all_gather | solution.py:421
  52.3 26.6 %collective-permute-start.1 = (f32[15,64,128]{2,1,0:T(8,128)}, f32[15,64,128]{2,1,0:T(8,128)}, u32[]{:S(2)}, u32[]{:S(2)}) collective-permute-start(f32[15,64,128]{2,1,0:T(8,128)} %bitcast.2.refs_0_), channel_id=1, source_target_pairs={{8,0},{9,1},{10,2},{11,3},{12,4},{13,5},{14,6},{15,7},{16,8},{17,9... | collective-permute-start | bytes 1474568 | tf_op jit(solution)/shard_map/ppermute | solution.py:384
  54.7 24.2 %collective-permute-start = (f32[15,64,128]{2,1,0:T(8,128)}, f32[15,64,128]{2,1,0:T(8,128)}, u32[]{:S(2)}, u32[]{:S(2)}) collective-permute-start(f32[15,64,128]{2,1,0:T(8,128)} %bitcast.2.refs_0_), channel_id=1, source_target_pairs={{0,8},{1,9},{2,10},{3,11},{4,12},{5,13},{6,14},{7,15},{8,16},{9,17... | collective-permute-start | bytes 1474568 | tf_op jit(solution)/shard_map/ppermute | solution.py:384
  59.7 20.5 %collective-permute-start.2 = (f32[15,64,128]{2,1,0:T(8,128)}, f32[15,64,128]{2,1,0:T(8,128)}, u32[]{:S(2)}, u32[]{:S(2)}) collective-permute-start(f32[15,64,128]{2,1,0:T(8,128)} %bitcast.2.refs_0_), channel_id=1, source_target_pairs={{0,2},{1,3},{2,4},{3,5},{4,6},{5,7},{6,0},{7,1},{8,10},{9,11},{10,... | collective-permute-start | bytes 1474568 | tf_op jit(solution)/shard_map/ppermute | solution.py:395
  61.1 23.8 %collective-permute-start.3 = (f32[15,64,128]{2,1,0:T(8,128)}, f32[15,64,128]{2,1,0:T(8,128)}, u32[]{:S(2)}, u32[]{:S(2)}) collective-permute-start(f32[15,64,128]{2,1,0:T(8,128)} %bitcast.2.refs_0_), channel_id=1, source_target_pairs={{0,4},{1,5},{2,6},{3,7},{4,0},{5,1},{6,2},{7,3},{8,12},{9,13},{10,... | collective-permute-start | bytes 1474568 | tf_op jit(solution)/shard_map/ppermute | solution.py:395
  63.5 21.4 %collective-permute-start.4 = (f32[15,64,128]{2,1,0:T(8,128)}, f32[15,64,128]{2,1,0:T(8,128)}, u32[]{:S(2)}, u32[]{:S(2)}) collective-permute-start(f32[15,64,128]{2,1,0:T(8,128)} %bitcast.2.refs_0_), channel_id=1, source_target_pairs={{0,6},{1,7},{2,0},{3,1},{4,2},{5,3},{6,4},{7,5},{8,14},{9,15},{10,... | collective-permute-start | bytes 1474568 | tf_op jit(solution)/shard_map/ppermute | solution.py:395
  69.1 1.6 copy-start
  84.9 49.2 %collective-permute-start.5 = (f32[30,64,128]{2,1,0:T(8,128)S(1)}, f32[30,64,128]{2,1,0:T(8,128)}, u32[]{:S(2)}, u32[]{:S(2)}) collective-permute-start(f32[30,64,128]{2,1,0:T(8,128)S(1)} %pad_maximum_fusion.refs_4_), channel_id=1, source_target_pairs={{0,2},{1,3},{2,4},{3,5},{4,6},{5,7},{6,0},{7,1},{8,10},{9,11},{10,... | collective-permute-start | bytes 2949128 | tf_op jit(solution)/shard_map/ppermute | solution.py:395
  86.7 47.4 %collective-permute-start.6 = (f32[30,64,128]{2,1,0:T(8,128)S(1)}, f32[30,64,128]{2,1,0:T(8,128)}, u32[]{:S(2)}, u32[]{:S(2)}) collective-permute-start(f32[30,64,128]{2,1,0:T(8,128)S(1)} %pad_maximum_fusion.refs_4_), channel_id=1, source_target_pairs={{0,4},{1,5},{2,6},{3,7},{4,0},{5,1},{6,2},{7,3},{8,12},{9,13},{10,... | collective-permute-start | bytes 2949128 | tf_op jit(solution)/shard_map/ppermute | solution.py:395
  89.1 45.0 %collective-permute-start.7 = (f32[30,64,128]{2,1,0:T(8,128)S(1)}, f32[30,64,128]{2,1,0:T(8,128)}, u32[]{:S(2)}, u32[]{:S(2)}) collective-permute-start(f32[30,64,128]{2,1,0:T(8,128)S(1)} %pad_maximum_fusion.refs_4_), channel_id=1, source_target_pairs={{0,6},{1,7},{2,0},{3,1},{4,2},{5,3},{6,4},{7,5},{8,14},{9,15},{10,... | collective-permute-start | bytes 2949128 | tf_op jit(solution)/shard_map/ppermute | solution.py:395
  89.9 1.2 copy-start.2
  91.1 51.1 %copy-start.9 = (s32[56,8]{0,1:T(8,128)S(1)}, s32[56,8]{0,1:T(8,128)}, u32[]{:S(2)}) copy-start(s32[56,8]{0,1:T(8,128)} %param.11) | copy-start | bytes 5380
  132.1 2.0 %copy-start.1 = (f32[126,64,64]{2,1,0:T(8,128)}, f32[126,64,64]{2,1,0:T(8,128)S(1)}, u32[]{:S(2)}) copy-start(f32[126,64,64]{2,1,0:T(8,128)S(1)} %get-tuple-element.78) | copy-start | bytes 6193156
  134.1 3.4 %collective-permute-start.8 = (f32[15,64,128]{2,1,0:T(8,128)}, f32[15,64,128]{2,1,0:T(8,128)S(1)}, u32[]{:S(2)}, u32[]{:S(2)}) collective-permute-start(f32[15,64,128]{2,1,0:T(8,128)} %bitcast.2.refs_0_), channel_id=1, source_target_pairs={{0,1},{1,0},{2,3},{3,2},{4,5},{5,4},{6,7},{7,6},{8,9},{9,8},{10,11... | collective-permute-start | bytes 1474568 | tf_op jit(solution)/shard_map/ppermute | solution.py:389
  135.8 3.1 %collective-permute-start.9 = (f32[15,64,128]{2,1,0:T(8,128)}, f32[15,64,128]{2,1,0:T(8,128)S(1)}, u32[]{:S(2)}, u32[]{:S(2)}) collective-permute-start(f32[15,64,128]{2,1,0:T(8,128)} %collective-permute-done.2.refs_1_), channel_id=1, source_target_pairs={{0,1},{1,0},{2,3},{3,2},{4,5},{5,4},{6,7},{7,6},{8,9},{9,8},{10,11... | collective-permute-start | bytes 1474568 | tf_op jit(solution)/shard_map/ppermute | solution.py:389
  135.9 5.1 %collective-permute-start.10 = (f32[15,64,128]{2,1,0:T(8,128)}, f32[15,64,128]{2,1,0:T(8,128)S(1)}, u32[]{:S(2)}, u32[]{:S(2)}) collective-permute-start(f32[15,64,128]{2,1,0:T(8,128)} %collective-permute-done.3.refs_2_), channel_id=1, source_target_pairs={{0,1},{1,0},{2,3},{3,2},{4,5},{5,4},{6,7},{7,6},{8,9},{9,8},{10,11... | collective-permute-start | bytes 1474568 | tf_op jit(solution)/shard_map/ppermute | solution.py:389
  136.3 11.5 %collective-permute-start.12 = (f32[30,64,128]{2,1,0:T(8,128)S(1)}, f32[30,64,128]{2,1,0:T(8,128)}, u32[]{:S(2)}, u32[]{:S(2)}) collective-permute-start(f32[30,64,128]{2,1,0:T(8,128)S(1)} %pad_maximum_fusion.refs_4_), channel_id=1, source_target_pairs={{0,1},{1,0},{2,3},{3,2},{4,5},{5,4},{6,7},{7,6},{8,9},{9,8},{10,11... | collective-permute-start | bytes 2949128 | tf_op jit(solution)/shard_map/ppermute | solution.py:389
  136.4 11.4 %collective-permute-start.13 = (f32[30,64,128]{2,1,0:T(8,128)}, f32[30,64,128]{2,1,0:T(8,128)}, u32[]{:S(2)}, u32[]{:S(2)}) collective-permute-start(f32[30,64,128]{2,1,0:T(8,128)} %collective-permute-done.5.refs_5_), channel_id=1, source_target_pairs={{0,1},{1,0},{2,3},{3,2},{4,5},{5,4},{6,7},{7,6},{8,9},{9,8},{10,11... | collective-permute-start | bytes 2949128 | tf_op jit(solution)/shard_map/ppermute | solution.py:389
  137.5 0.8 copy-start.3
  138.3 9.6 %collective-permute-start.14 = (f32[30,64,128]{2,1,0:T(8,128)}, f32[30,64,128]{2,1,0:T(8,128)}, u32[]{:S(2)}, u32[]{:S(2)}) collective-permute-start(f32[30,64,128]{2,1,0:T(8,128)} %collective-permute-done.6.refs_6_), channel_id=1, source_target_pairs={{0,1},{1,0},{2,3},{3,2},{4,5},{5,4},{6,7},{7,6},{8,9},{9,8},{10,11... | collective-permute-start | bytes 2949128 | tf_op jit(solution)/shard_map/ppermute | solution.py:389
  138.9 0.8 copy-start.5
  139.8 8.1 %collective-permute-start.15 = (f32[30,64,128]{2,1,0:T(8,128)}, f32[30,64,128]{2,1,0:T(8,128)}, u32[]{:S(2)}, u32[]{:S(2)}) collective-permute-start(f32[30,64,128]{2,1,0:T(8,128)} %collective-permute-done.7.refs_7_), channel_id=1, source_target_pairs={{0,1},{1,0},{2,3},{3,2},{4,5},{5,4},{6,7},{7,6},{8,9},{9,8},{10,11... | collective-permute-start | bytes 2949128 | tf_op jit(solution)/shard_map/ppermute | solution.py:389
  141.0 0.8 copy-start.7
  141.8 6.0 %collective-permute-start.11 = (f32[15,64,128]{2,1,0:T(8,128)}, f32[15,64,128]{2,1,0:T(8,128)}, u32[]{:S(2)}, u32[]{:S(2)}) collective-permute-start(f32[15,64,128]{2,1,0:T(8,128)} %collective-permute-done.4.refs_3_), channel_id=1, source_target_pairs={{0,1},{1,0},{2,3},{3,2},{4,5},{5,4},{6,7},{7,6},{8,9},{9,8},{10,11... | collective-permute-start | bytes 1474568 | tf_op jit(solution)/shard_map/ppermute | solution.py:389
  147.9 1.0 copy-start.4
  148.9 1.0 copy-start.6
  150.0 1.0 copy-start.8
Sparse Core Ops, SparseCore 0:
  32.4 43.8 all-gather.2

commit v4 on v3

--- a/solution.py
+++ b/solution.py
@@ -57,12 +57,12 @@
     return pltpu.CompilerParams(vmem_limit_bytes=mib * MIB)
 
 
-def load_lanes(g_ref, w_ref):
+def load_lanes(g_ref, w_ref, amount):
     place = lax.broadcasted_iota(jnp.int32, (RANK, 128), 0)
 
     def body(i, carry):
-        block = g_ref[pl.ds(i, 128, stride=RANK), :].T
-        w_ref[i, 0:RANK, :] = block[0:RANK]
+        block = g_ref[pl.ds(i, amount, stride=RANK), :].T
+        w_ref[i, 0:RANK, 0:amount] = block[0:RANK]
         w_ref[i, RANK:128, :] = jnp.where(place == i, 1.0, 0.0).astype(F32)
         return carry
 
@@ -160,7 +160,7 @@
     return pl.pallas_call(
         gram_kernel,
         out_shape=(
-            jax.ShapeDtypeStruct((128 * RANK, 128), F32),
+            jax.ShapeDtypeStruct((RANK * RANK, 128), F32),
             jax.ShapeDtypeStruct((32, 128), F32),
         ),
         in_specs=[pl.BlockSpec(memory_space=pl.ANY)] * 2,
@@ -176,7 +176,7 @@
 
 
 def factor_kernel(g_ref, um_ref, unit_ref, w_ref):
-    load_lanes(g_ref, w_ref)
+    load_lanes(g_ref, w_ref, RANK)
     eliminate(w_ref)
     place = lax.broadcasted_iota(jnp.int32, (RANK, 128), 0)
     rows = w_ref.reshape(RANK * 128, 128)
@@ -267,7 +267,7 @@
         begin = 2**level - 1
         lax.fori_loop(begin, 2 * begin + 1, join, 0, unroll=min(2**level, 16))
     g_ref[TOPN * RANK :, :] = jnp.zeros_like(g_ref[TOPN * RANK :, :])
-    load_lanes(g_ref, w_ref)
+    load_lanes(g_ref, w_ref, 128)
     eliminate(w_ref)
     store_lanes(w_ref, um_ref, 128)
 
@@ -302,7 +302,7 @@
             pltpu.VMEM((RANK, 128, 128), F32),
             pltpu.VMEM((128 * RANK, 128), F32),
         ],
-        compiler_params=params(48),
+        compiler_params=params(62),
         cost_estimate=cost(42),
         name="top_tree",
     )(own, c, e, p)
@@ -372,7 +372,7 @@
             ],
         ),
         out_shape=jax.ShapeDtypeStruct((ROW, CPL, RANK, RANK), F32),
-        compiler_params=params(28),
+        compiler_params=params(62),
         cost_estimate=cost(32),
         name="couple",
     )(where, s, um, *pieces)
@@ -429,13 +429,13 @@
     new_leaves, moved = apply_call(um, leaf_bases, transfers, top_transfers)
     pair = jnp.concatenate([before, after], axis=0)
     pair, moved, um, *line = together(pair, moved, um, *line)
+    line_other = [swapped(part) for part in line]
     sides = [pair] + [turned_column(pair, by) for by in (1, 2, 3)]
     new_top, root_factor, mine = top_call(
         own.reshape(1), frontier, top_transfers, moved[NODES - 1]
     )
-    mine, *rest = together(mine, *line, *sides)
-    line, sides = rest[0:4], rest[4:8]
-    line_other = [swapped(part) for part in line]
+    mine, *rest = together(mine, *line_other, *sides)
+    line_other, sides = rest[0:4], rest[4:8]
     sides_other = [swapped(part) for part in sides]
     new_transfers = moved.at[NODES - 1].set(mine)
     new_couplings = couple_call(where, couplings, um, line + sides + line_other + sides_other)

time: 188 us -> 180 us (0.957)
  local copies, waits for them, and re-layouts: 22.1 us -> 17.4 us
  Pallas kernels: 109 us -> 107 us
  waiting for transfers between devices: 6.63 us -> 4.7 us
    unnamed x23, local copies, waits for them, and re-layouts: 20.7 us -> 15.4 us
    pallas_call x1, Pallas kernels: 20.1 us -> 16.2 us  [factor_call(): pl.pallas_call(factor_kernel, out_shape=(jax.ShapeDtypeStruct((RANK * RAN...]
  transfers between devices with their start and end apart: 17 -> 17, of which waited for: 4 -> 1; matrix products, arithmetic and copies ran while one was open for 7% -> 8% of each run, Pallas kernels for 37% -> 37%
where the time goes in v4:
time: 180 us
  Pallas kernels  107 us (59%)
  starting transfers between devices  18.9 us (10%)
  local copies, waits for them, and re-layouts  17.4 us (10%)
  blocking collectives  14.7 us (8%)
  between operations  14.2 us (8%)
  waiting for transfers between devices  4.7 us (3%)
  other arithmetic  2.46 us (1%)
    pallas_call x1, Pallas kernels, top_call(): pl.pallas_call(top_kernel, in_specs=[pl.BlockSpec(memory_space=pltpu.SMEM...  42.7 us
    pallas_call x1, Pallas kernels, couple_call(): pl.pallas_call(couple_kernel, grid_spec=pltpu.PrefetchScalarGridSpec(num_...  31.4 us
    pallas_call x1, Pallas kernels, factor_call(): pl.pallas_call(factor_kernel, out_shape=(jax.ShapeDtypeStruct((RANK * RAN...  16.2 us
    unnamed x23, local copies, waits for them, and re-layouts  15.4 us
    all_gather x1, blocking collectives, on_device(): lax.all_gather(carried, 'leaf', axis_index_groups=along, axis=0, tiled=Fa...  14.7 us
    pallas_call x1, Pallas kernels, gram_call(): pl.pallas_call(gram_kernel, out_shape=(jax.ShapeDtypeStruct((RANK * RANK,...  8.85 us
    pallas_call x1, Pallas kernels, apply_call(): pl.pallas_call(apply_kernel, in_specs=[vm, vm, vm, pl.BlockSpec(memory_sp...  8.19 us
    ppermute x2, starting transfers between devices, shifted(): return lax.ppermute(array, axis, pairs)  7.39 us
  transfers between devices with their start and end apart: 17, of which 1 were waited for; matrix products, arithmetic and copies ran while one was open for 8% of the time, Pallas kernels for 37%

profile of v4, /device:TPU:7, one launch (start us, length us, event | category | flops | bytes accessed | tf_op | source)
XLA Modules:
  0.0 179.6 jit_solution(17636692409189140038)
XLA Ops:
  7.2 0.0 all-gather.3.cloned.1.call-start
  7.2 8.8 %gram_up.1 = (f32[4096,128]{1,0:T(8,128)}, f32[32,128]{1,0:T(8,128)}) custom-call(f32[32,64,256]{2,1,0:T(8,128)} %v_ref.1, f32[63,64,64]{2,1,0:T(8,128)} %e_ref.2), custom_call_target="tpu_custom_call" | custom-call | flops 12000000 | bytes 30000000 | tf_op jit(solution)/shard_map/gram_up/pallas_call | solution.py:160
  16.1 14.7 %all-gather = f32[256,128]{1,0:T(8,128)S(1)} all-gather(f32[32,128]{1,0:T(8,128)} %get-tuple-element.44), channel_id=2, replica_groups={{0,1,2,3,4,5,6,7},{8,9,10,11,12,13,14,15},{16,17,18,19,20,21,22,23},{24..., dimensions={0}, use_global_device_ids=true | all-gather | bytes 147456 | tf_op jit(solution)/shard_map/all_gather | solution.py:418
  30.7 0.6 slice_add_fusion
  31.4 0.0 all-gather.3.cloned.1.call-update
  31.4 0.0 copy-start.2
  31.4 1.6 copy-done.2
  33.0 16.2 %factor_local.1 = (f32[4096,128]{1,0:T(8,128)S(1)}, f32[960,128]{1,0:T(8,128)S(1)}) custom-call(f32[4096,128]{1,0:T(8,128)S(1)} %copy-done.2), custom_call_target="tpu_custom_call" | custom-call | flops 15000000 | bytes 37500000 | tf_op jit(solution)/shard_map/factor_local/pallas_call | solution.py:199
  49.2 0.0 copy-start
  49.2 0.0 copy-start.3
  49.2 2.5 %collective-permute-start.1 = (f32[15,64,128]{2,1,0:T(8,128)S(1)}, f32[15,64,128]{2,1,0:T(8,128)S(1)}, u32[]{:S(2)}, u32[]{:S(2)}) collective-permute-start(f32[15,64,128]{2,1,0:T(8,128)S(1)} %bitcast.10), channel_id=1, source_target_pairs={{8,0},{9,1},{10,2},{11,3},{12,4},{13,5},{14,6},{15,7},{16,8},{17,9... | collective-permute-start | bytes 1474568 | tf_op jit(solution)/shard_map/ppermute | solution.py:384
  51.7 4.9 %collective-permute-start = (f32[15,64,128]{2,1,0:T(8,128)S(1)}, f32[15,64,128]{2,1,0:T(8,128)}, u32[]{:S(2)}, u32[]{:S(2)}) collective-permute-start(f32[15,64,128]{2,1,0:T(8,128)S(1)} %bitcast.11), channel_id=1, source_target_pairs={{0,8},{1,9},{2,10},{3,11},{4,12},{5,13},{6,14},{7,15},{8,16},{9,17... | collective-permute-start | bytes 1474568 | tf_op jit(solution)/shard_map/ppermute | solution.py:384
  56.6 1.4 collective-permute-start.2
  58.1 2.4 %collective-permute-start.3 = (f32[15,64,128]{2,1,0:T(8,128)S(1)}, f32[15,64,128]{2,1,0:T(8,128)}, u32[]{:S(2)}, u32[]{:S(2)}) collective-permute-start(f32[15,64,128]{2,1,0:T(8,128)S(1)} %bitcast.13), channel_id=1, source_target_pairs={{0,4},{1,5},{2,6},{3,7},{4,0},{5,1},{6,2},{7,3},{8,12},{9,13},{10,... | collective-permute-start | bytes 1474568 | tf_op jit(solution)/shard_map/ppermute | solution.py:395
  60.5 0.1 collective-permute-start.4
  60.5 5.5 %copy.16.top_ref.e_ref = f32[126,64,64]{2,1,0:T(8,128)} copy(f32[126,64,64]{0,2,1:T(8,128)} %param.9) | data formatting | bytes 4128768 | tf_op args[2]
  66.1 0.0 copy-done
  66.1 0.0 copy-start.1
  66.1 1.6 copy-done.1
  67.7 8.2 %apply_local.1 = (f32[32,64,256]{2,1,0:T(8,128)}, f32[63,64,64]{2,1,0:T(8,128)}) custom-call(f32[64,64,128]{2,1,0:T(8,128)S(1)} %bitcast.8, f32[32,64,256]{2,1,0:T(8,128)} %v_ref.1, f32[63,64,64]{2,1,0:T(8,128)S(1)} %copy-done.1, f32[126,64,64]{2,1,0:T(8,128)} %copy.16.top_ref.e_ref), custom_call_target="tpu_custom_call" | custom-call | flops 9000000 | bytes 22500000 | tf_op jit(solution)/shard_map/apply_local/pallas_call | solution.py:236
  75.9 0.0 collective-permute-done.1
  75.9 0.0 collective-permute-done
  75.9 1.1 pad_maximum_fusion.refs_4_
  77.0 0.0 copy-start.4
  77.0 0.0 collective-permute-done.2.refs_1_
  77.0 4.6 %collective-permute-done.3.refs_2_ = f32[15,64,128]{2,1,0:T(8,128)} collective-permute-done((f32[15,64,128]{2,1,0:T(8,128)S(1)}, f32[15,64,128]{2,1,0:T(8,128)}, u32[]{:S(2)}, u32[]{:S(2)}) %collective-permute-start.3) | collective-permute-done | bytes 491552 | tf_op jit(solution)/shard_map/ppermute | solution.py:395
  81.7 0.0 collective-permute-done.4.refs_3_
  81.7 0.0 copy-done.3
  81.7 1.6 collective-permute-start.5
  83.3 0.1 collective-permute-start.6
  83.4 0.6 collective-permute-start.9
  84.0 2.4 %collective-permute-start.10 = (f32[30,64,128]{2,1,0:T(8,128)S(1)}, f32[30,64,128]{2,1,0:T(8,128)}, u32[]{:S(2)}, u32[]{:S(2)}) collective-permute-start(f32[30,64,128]{2,1,0:T(8,128)S(1)} %pad_maximum_fusion.refs_4_), channel_id=1, source_target_pairs={{0,4},{1,5},{2,6},{3,7},{4,0},{5,1},{6,2},{7,3},{8,12},{9,13},{10,... | collective-permute-start | bytes 2949128 | tf_op jit(solution)/shard_map/ppermute | solution.py:395
  86.4 0.3 collective-permute-start.11
  86.7 0.0 collective-permute-done.5.refs_8_
  86.7 0.8 copy-done.7
  87.5 1.3 collective-permute-start.7
  88.8 0.0 collective-permute-done.6.refs_9_
  88.8 0.0 collective-permute-start.8
  88.8 1.4 slice_bitcast_fusion.p_ref
  90.2 42.7 %top_tree.1 = (f32[126,64,64]{2,1,0:T(8,128)}, f32[64,64]{1,0:T(8,128)}, f32[64,64]{1,0:T(8,128)}) custom-call(s32[1]{0:T(128)} %bitcast.3.own_ref, f32[64,32,128]{2,1,0:T(8,128)} %all-gather.3.cloned.1.call-done.c_ref, f32[126,64,64]{2,1,0:T(8,128)} %copy.16.top_ref.e_ref, f32[64,64]{1,0:T(8,128)} %slice_bitcast_fusion.p_ref), custom_call_target="tpu_custom_call" | custom-call | flops 42000000 | bytes 105000000 | tf_op jit(solution)/shard_map/top_tree/pallas_call | solution.py:292
  132.9 0.0 collective-permute-done.7.refs_10_
  132.9 0.0 collective-permute-done.8.refs_11_
  132.9 0.0 collective-permute-done.9.refs_5_
  132.9 0.0 copy-start.5
  132.9 0.0 collective-permute-done.10.refs_6_
  132.9 0.0 collective-permute-done.11.refs_7_
  132.9 0.0 copy-done.4
  132.9 0.6 collective-permute-start.12
  133.5 0.1 collective-permute-start.13
  133.6 0.4 collective-permute-start.14
  134.0 0.1 collective-permute-start.15
  134.1 0.0 copy-done.9
  134.1 0.1 copy.18
  134.2 0.7 fusion.8.where_ref
  134.9 4.8 %copy.21 = f32[126,64,64]{0,2,1:T(8,128)} copy(f32[126,64,64]{2,1,0:T(8,128)} %get-tuple-element.78) | data formatting | bytes 4128768
  139.8 0.0 copy-done.5
  139.8 0.0 copy-done.8
  139.8 0.6 bitcast_dynamic-update-slice_fusion
  140.4 0.0 collective-permute-done.12.refs_12_
  140.4 0.0 collective-permute-done.13.refs_13_
  140.4 1.0 copy-done.6
  141.3 0.0 collective-permute-done.14.refs_14_
  141.3 0.0 collective-permute-done.15.refs_15_
  141.3 31.4 %couple.1 = f32[56,8,64,64]{3,2,1,0:T(8,128)} custom-call(s32[56,8]{1,0:T(8,128)} %fusion.8.where_ref, f32[56,8,64,64]{3,2,1,0:T(8,128)} %s_ref.1, f32[64,64,128]{2,1,0:T(8,128)} %bitcast.9, f32[15,64,128]{2,1,0:T(8,128)} %bitcast.16, f32[15,64,128]{2,1,0:T(8,128)} %collective-permute-done.2.refs_1_, f32[15,64,128]{2,1,0:T(8,128)} %collective-permute-done.3.refs_2_, ...), custom_call_target="tpu_custom_call" | custom-call | flops 32000000 | bytes 80000000 | tf_op jit(solution)/shard_map/couple/pallas_call | solution.py:361
  (5 shorter events, 0.0 us)
Async XLA Ops:
  7.2 83.0 %all-gather.3.cloned.1.call-start = ((), (), s32[]{:S(2)}) async-start(), calls=%async_computation | async-start | bytes 1114112 | tf_op jit(solution)/shard_map/all_gather | solution.py:421
  31.4 1.6 copy-start.2
  49.2 16.9 %copy-start = (f32[4096,128]{1,0:T(8,128)}, f32[4096,128]{1,0:T(8,128)S(1)}, u32[]{:S(2)}) copy-start(f32[4096,128]{1,0:T(8,128)S(1)} %get-tuple-element.47) | copy-start | bytes 6291460
  49.2 32.4 %copy-start.3 = (f32[960,128]{1,0:T(8,128)}, f32[960,128]{1,0:T(8,128)S(1)}, u32[]{:S(2)}) copy-start(f32[960,128]{1,0:T(8,128)S(1)} %get-tuple-element.49) | copy-start | bytes 1474564
  49.2 26.6 %collective-permute-start.1 = (f32[15,64,128]{2,1,0:T(8,128)S(1)}, f32[15,64,128]{2,1,0:T(8,128)S(1)}, u32[]{:S(2)}, u32[]{:S(2)}) collective-permute-start(f32[15,64,128]{2,1,0:T(8,128)S(1)} %bitcast.10), channel_id=1, source_target_pairs={{8,0},{9,1},{10,2},{11,3},{12,4},{13,5},{14,6},{15,7},{16,8},{17,9... | collective-permute-start | bytes 1474568 | tf_op jit(solution)/shard_map/ppermute | solution.py:384
  51.7 24.2 %collective-permute-start = (f32[15,64,128]{2,1,0:T(8,128)S(1)}, f32[15,64,128]{2,1,0:T(8,128)}, u32[]{:S(2)}, u32[]{:S(2)}) collective-permute-start(f32[15,64,128]{2,1,0:T(8,128)S(1)} %bitcast.11), channel_id=1, source_target_pairs={{0,8},{1,9},{2,10},{3,11},{4,12},{5,13},{6,14},{7,15},{8,16},{9,17... | collective-permute-start | bytes 1474568 | tf_op jit(solution)/shard_map/ppermute | solution.py:384
  56.6 20.4 %collective-permute-start.2 = (f32[15,64,128]{2,1,0:T(8,128)S(1)}, f32[15,64,128]{2,1,0:T(8,128)}, u32[]{:S(2)}, u32[]{:S(2)}) collective-permute-start(f32[15,64,128]{2,1,0:T(8,128)S(1)} %bitcast.12), channel_id=1, source_target_pairs={{0,2},{1,3},{2,4},{3,5},{4,6},{5,7},{6,0},{7,1},{8,10},{9,11},{10,... | collective-permute-start | bytes 1474568 | tf_op jit(solution)/shard_map/ppermute | solution.py:395
  58.1 23.6 %collective-permute-start.3 = (f32[15,64,128]{2,1,0:T(8,128)S(1)}, f32[15,64,128]{2,1,0:T(8,128)}, u32[]{:S(2)}, u32[]{:S(2)}) collective-permute-start(f32[15,64,128]{2,1,0:T(8,128)S(1)} %bitcast.13), channel_id=1, source_target_pairs={{0,4},{1,5},{2,6},{3,7},{4,0},{5,1},{6,2},{7,3},{8,12},{9,13},{10,... | collective-permute-start | bytes 1474568 | tf_op jit(solution)/shard_map/ppermute | solution.py:395
  60.5 21.2 %collective-permute-start.4 = (f32[15,64,128]{2,1,0:T(8,128)S(1)}, f32[15,64,128]{2,1,0:T(8,128)}, u32[]{:S(2)}, u32[]{:S(2)}) collective-permute-start(f32[15,64,128]{2,1,0:T(8,128)S(1)} %bitcast.14), channel_id=1, source_target_pairs={{0,6},{1,7},{2,0},{3,1},{4,2},{5,3},{6,4},{7,5},{8,14},{9,15},{10,... | collective-permute-start | bytes 1474568 | tf_op jit(solution)/shard_map/ppermute | solution.py:395
  66.1 1.6 copy-start.1
  77.0 55.9 %copy-start.4 = (f32[30,64,128]{2,1,0:T(8,128)}, f32[30,64,128]{2,1,0:T(8,128)S(1)}, u32[]{:S(2)}) copy-start(f32[30,64,128]{2,1,0:T(8,128)S(1)} %pad_maximum_fusion.refs_4_) | copy-start | bytes 2949124
  81.7 5.0 %collective-permute-start.5 = (f32[15,64,128]{2,1,0:T(8,128)S(1)}, f32[15,64,128]{2,1,0:T(8,128)S(1)}, u32[]{:S(2)}, u32[]{:S(2)}) collective-permute-start(f32[15,64,128]{2,1,0:T(8,128)S(1)} %bitcast.15), channel_id=1, source_target_pairs={{0,1},{1,0},{2,3},{3,2},{4,5},{5,4},{6,7},{7,6},{8,9},{9,8},{10,11... | collective-permute-start | bytes 1474568 | tf_op jit(solution)/shard_map/ppermute | solution.py:389
  83.3 5.5 %collective-permute-start.6 = (f32[15,64,128]{2,1,0:T(8,128)}, f32[15,64,128]{2,1,0:T(8,128)}, u32[]{:S(2)}, u32[]{:S(2)}) collective-permute-start(f32[15,64,128]{2,1,0:T(8,128)} %collective-permute-done.2.refs_1_), channel_id=1, source_target_pairs={{0,1},{1,0},{2,3},{3,2},{4,5},{5,4},{6,7},{7,6},{8,9},{9,8},{10,11... | collective-permute-start | bytes 1474568 | tf_op jit(solution)/shard_map/ppermute | solution.py:389
  83.4 49.5 %collective-permute-start.9 = (f32[30,64,128]{2,1,0:T(8,128)S(1)}, f32[30,64,128]{2,1,0:T(8,128)S(1)}, u32[]{:S(2)}, u32[]{:S(2)}) collective-permute-start(f32[30,64,128]{2,1,0:T(8,128)S(1)} %pad_maximum_fusion.refs_4_), channel_id=1, source_target_pairs={{0,2},{1,3},{2,4},{3,5},{4,6},{5,7},{6,0},{7,1},{8,10},{9,11},{10,... | collective-permute-start | bytes 2949128 | tf_op jit(solution)/shard_map/ppermute | solution.py:395
  84.0 48.9 %collective-permute-start.10 = (f32[30,64,128]{2,1,0:T(8,128)S(1)}, f32[30,64,128]{2,1,0:T(8,128)}, u32[]{:S(2)}, u32[]{:S(2)}) collective-permute-start(f32[30,64,128]{2,1,0:T(8,128)S(1)} %pad_maximum_fusion.refs_4_), channel_id=1, source_target_pairs={{0,4},{1,5},{2,6},{3,7},{4,0},{5,1},{6,2},{7,3},{8,12},{9,13},{10,... | collective-permute-start | bytes 2949128 | tf_op jit(solution)/shard_map/ppermute | solution.py:395
  86.4 46.5 %collective-permute-start.11 = (f32[30,64,128]{2,1,0:T(8,128)S(1)}, f32[30,64,128]{2,1,0:T(8,128)}, u32[]{:S(2)}, u32[]{:S(2)}) collective-permute-start(f32[30,64,128]{2,1,0:T(8,128)S(1)} %pad_maximum_fusion.refs_4_), channel_id=1, source_target_pairs={{0,6},{1,7},{2,0},{3,1},{4,2},{5,3},{6,4},{7,5},{8,14},{9,15},{10,... | collective-permute-start | bytes 2949128 | tf_op jit(solution)/shard_map/ppermute | solution.py:395
  86.7 0.8 copy-start.7
  87.5 45.4 %collective-permute-start.7 = (f32[15,64,128]{2,1,0:T(8,128)}, f32[15,64,128]{2,1,0:T(8,128)}, u32[]{:S(2)}, u32[]{:S(2)}) collective-permute-start(f32[15,64,128]{2,1,0:T(8,128)} %collective-permute-done.3.refs_2_), channel_id=1, source_target_pairs={{0,1},{1,0},{2,3},{3,2},{4,5},{5,4},{6,7},{7,6},{8,9},{9,8},{10,11... | collective-permute-start | bytes 1474568 | tf_op jit(solution)/shard_map/ppermute | solution.py:389
  88.8 44.1 %collective-permute-start.8 = (f32[15,64,128]{2,1,0:T(8,128)}, f32[15,64,128]{2,1,0:T(8,128)}, u32[]{:S(2)}, u32[]{:S(2)}) collective-permute-start(f32[15,64,128]{2,1,0:T(8,128)} %collective-permute-done.4.refs_3_), channel_id=1, source_target_pairs={{0,1},{1,0},{2,3},{3,2},{4,5},{5,4},{6,7},{7,6},{8,9},{9,8},{10,11... | collective-permute-start | bytes 1474568 | tf_op jit(solution)/shard_map/ppermute | solution.py:389
  90.2 43.9 %copy-start.9 = (s32[56,8]{0,1:T(8,128)S(1)}, s32[56,8]{0,1:T(8,128)}, u32[]{:S(2)}) copy-start(s32[56,8]{0,1:T(8,128)} %param.11) | copy-start | bytes 5380
  132.9 6.9 %copy-start.5 = (f32[30,64,128]{2,1,0:T(8,128)}, f32[30,64,128]{2,1,0:T(8,128)S(1)}, u32[]{:S(2)}) copy-start(f32[30,64,128]{2,1,0:T(8,128)S(1)} %collective-permute-done.9.refs_5_) | copy-start | bytes 2949124
  132.9 7.5 %collective-permute-start.12 = (f32[30,64,128]{2,1,0:T(8,128)S(1)}, f32[30,64,128]{2,1,0:T(8,128)S(1)}, u32[]{:S(2)}, u32[]{:S(2)}) collective-permute-start(f32[30,64,128]{2,1,0:T(8,128)S(1)} %pad_maximum_fusion.refs_4_), channel_id=1, source_target_pairs={{0,1},{1,0},{2,3},{3,2},{4,5},{5,4},{6,7},{7,6},{8,9},{9,8},{10,11... | collective-permute-start | bytes 2949128 | tf_op jit(solution)/shard_map/ppermute | solution.py:389
  133.5 6.9 %collective-permute-start.13 = (f32[30,64,128]{2,1,0:T(8,128)S(1)}, f32[30,64,128]{2,1,0:T(8,128)}, u32[]{:S(2)}, u32[]{:S(2)}) collective-permute-start(f32[30,64,128]{2,1,0:T(8,128)S(1)} %collective-permute-done.9.refs_5_), channel_id=1, source_target_pairs={{0,1},{1,0},{2,3},{3,2},{4,5},{5,4},{6,7},{7,6},{8,9},{9,8},{10,11... | collective-permute-start | bytes 2949128 | tf_op jit(solution)/shard_map/ppermute | solution.py:389
  133.6 7.8 %collective-permute-start.14 = (f32[30,64,128]{2,1,0:T(8,128)}, f32[30,64,128]{2,1,0:T(8,128)}, u32[]{:S(2)}, u32[]{:S(2)}) collective-permute-start(f32[30,64,128]{2,1,0:T(8,128)} %collective-permute-done.10.refs_6_), channel_id=1, source_target_pairs={{0,1},{1,0},{2,3},{3,2},{4,5},{5,4},{6,7},{7,6},{8,9},{9,8},{10,11... | collective-permute-start | bytes 2949128 | tf_op jit(solution)/shard_map/ppermute | solution.py:389
  134.0 7.3 %collective-permute-start.15 = (f32[30,64,128]{2,1,0:T(8,128)}, f32[30,64,128]{2,1,0:T(8,128)}, u32[]{:S(2)}, u32[]{:S(2)}) collective-permute-start(f32[30,64,128]{2,1,0:T(8,128)} %collective-permute-done.11.refs_7_), channel_id=1, source_target_pairs={{0,1},{1,0},{2,3},{3,2},{4,5},{5,4},{6,7},{7,6},{8,9},{9,8},{10,11... | collective-permute-start | bytes 2949128 | tf_op jit(solution)/shard_map/ppermute | solution.py:389
  134.9 4.8 %copy-start.8 = (f32[64,64]{1,0:T(8,128)S(1)}, f32[64,64]{1,0:T(8,128)}, u32[]{:S(2)}) copy-start(f32[64,64]{1,0:T(8,128)} %get-tuple-element.59) | copy-start | bytes 49156
  140.4 1.0 copy-start.6
Sparse Core Ops, SparseCore 0:
  31.5 43.7 all-gather.2

commit v5 on v4

--- a/solution.py
+++ b/solution.py
@@ -17,7 +17,7 @@
 COLUMN = 8
 TOPN = 127
 ROWS_STEP = 8
-UNROLL = 4
+UNROLL = 8
 CHUNKS = 4
 MIB = 1024 * 1024
 F32 = jnp.float32
@@ -265,7 +265,7 @@
 
     for level in range(5, -1, -1):
         begin = 2**level - 1
-        lax.fori_loop(begin, 2 * begin + 1, join, 0, unroll=min(2**level, 16))
+        lax.fori_loop(begin, 2 * begin + 1, join, 0, unroll=2**level)
     g_ref[TOPN * RANK :, :] = jnp.zeros_like(g_ref[TOPN * RANK :, :])
     load_lanes(g_ref, w_ref, 128)
     eliminate(w_ref)
@@ -281,7 +281,7 @@
         new_ref[c] = q[RANK:128]
         return carry
 
-    lax.fori_loop(0, 63, out, 0, unroll=9)
+    lax.fori_loop(0, 63, out, 0, unroll=21)
     root_ref[...] = um_ref[0:RANK, 0:RANK]
     up = um_ref[block_at(63 + own_ref[0] // 2), RANK:128]
     mine_ref[...] = mul3(p_ref[...], up, NT)

time: 180 us -> 175 us (0.972)
  Pallas kernels: 107 us -> 93 us
  waiting for transfers between devices: 4.7 us -> 12.7 us
    pallas_call x1, Pallas kernels: 42.7 us -> 30.8 us  [top_call(): pl.pallas_call(top_kernel, in_specs=[pl.BlockSpec(memory_space=pltpu.SMEM...]
    ppermute x6, waiting for transfers between devices: 4.66 us -> 12.6 us  [turned_column(): return lax.ppermute(array, 'leaf', pairs)]
    pallas_call x1, Pallas kernels: 31.4 us -> 29 us  [couple_call(): pl.pallas_call(couple_kernel, grid_spec=pltpu.PrefetchScalarGridSpec(num_...]
  transfers between devices with their start and end apart: 17 -> 17, of which waited for: 1 -> 2; matrix products, arithmetic and copies ran while one was open for 8% -> 8% of each run, Pallas kernels for 37% -> 32%
where the time goes in v5:
time: 175 us; the launch traced here: 174 us
  Pallas kernels  93 us (53%)
  starting transfers between devices  19.8 us (11%)
  local copies, waits for them, and re-layouts  17.4 us (10%)
  blocking collectives  14.7 us (8%)
  between operations  14.2 us (8%)
  waiting for transfers between devices  12.7 us (7%)
  other arithmetic  2.46 us (1%)
    pallas_call x1, Pallas kernels, top_call(): pl.pallas_call(top_kernel, in_specs=[pl.BlockSpec(memory_space=pltpu.SMEM...  30.8 us
    pallas_call x1, Pallas kernels, couple_call(): pl.pallas_call(couple_kernel, grid_spec=pltpu.PrefetchScalarGridSpec(num_...  29 us
    pallas_call x1, Pallas kernels, factor_call(): pl.pallas_call(factor_kernel, out_shape=(jax.ShapeDtypeStruct((RANK * RAN...  16.2 us
    unnamed x23, local copies, waits for them, and re-layouts  15.4 us
    all_gather x1, blocking collectives, on_device(): lax.all_gather(carried, 'leaf', axis_index_groups=along, axis=0, tiled=Fa...  14.7 us
    ppermute x6, waiting for transfers between devices, turned_column(): return lax.ppermute(array, 'leaf', pairs)  12.6 us
    pallas_call x1, Pallas kernels, gram_call(): pl.pallas_call(gram_kernel, out_shape=(jax.ShapeDtypeStruct((RANK * RANK,...  8.85 us
    pallas_call x1, Pallas kernels, apply_call(): pl.pallas_call(apply_kernel, in_specs=[vm, vm, vm, pl.BlockSpec(memory_sp...  8.19 us
  transfers between devices with their start and end apart: 17, of which 2 were waited for; matrix products, arithmetic and copies ran while one was open for 8% of the time, Pallas kernels for 32%

profile of v5, /device:TPU:7, one launch (start us, length us, event | category | flops | bytes accessed | tf_op | source)
XLA Modules:
  0.0 174.2 jit_solution(12144649984031405075)
XLA Ops:
  7.2 0.0 all-gather.3.cloned.1.call-start
  7.2 8.8 %gram_up.1 = (f32[4096,128]{1,0:T(8,128)}, f32[32,128]{1,0:T(8,128)}) custom-call(f32[32,64,256]{2,1,0:T(8,128)} %v_ref.1, f32[63,64,64]{2,1,0:T(8,128)} %e_ref.2), custom_call_target="tpu_custom_call" | custom-call | flops 12000000 | bytes 30000000 | tf_op jit(solution)/shard_map/gram_up/pallas_call | solution.py:160
  16.1 14.7 %all-gather = f32[256,128]{1,0:T(8,128)S(1)} all-gather(f32[32,128]{1,0:T(8,128)} %get-tuple-element.44), channel_id=2, replica_groups={{0,1,2,3,4,5,6,7},{8,9,10,11,12,13,14,15},{16,17,18,19,20,21,22,23},{24..., dimensions={0}, use_global_device_ids=true | all-gather | bytes 147456 | tf_op jit(solution)/shard_map/all_gather | solution.py:418
  30.7 0.6 slice_add_fusion
  31.4 0.0 all-gather.3.cloned.1.call-update
  31.4 0.0 copy-start.2
  31.4 1.6 copy-done.2
  33.0 16.2 %factor_local.1 = (f32[4096,128]{1,0:T(8,128)S(1)}, f32[960,128]{1,0:T(8,128)S(1)}) custom-call(f32[4096,128]{1,0:T(8,128)S(1)} %copy-done.2), custom_call_target="tpu_custom_call" | custom-call | flops 15000000 | bytes 37500000 | tf_op jit(solution)/shard_map/factor_local/pallas_call | solution.py:199
  49.2 0.0 copy-start
  49.2 0.0 copy-start.3
  49.2 2.5 %collective-permute-start.1 = (f32[15,64,128]{2,1,0:T(8,128)S(1)}, f32[15,64,128]{2,1,0:T(8,128)S(1)}, u32[]{:S(2)}, u32[]{:S(2)}) collective-permute-start(f32[15,64,128]{2,1,0:T(8,128)S(1)} %bitcast.10), channel_id=1, source_target_pairs={{8,0},{9,1},{10,2},{11,3},{12,4},{13,5},{14,6},{15,7},{16,8},{17,9... | collective-permute-start | bytes 1474568 | tf_op jit(solution)/shard_map/ppermute | solution.py:384
  51.7 4.9 %collective-permute-start = (f32[15,64,128]{2,1,0:T(8,128)S(1)}, f32[15,64,128]{2,1,0:T(8,128)}, u32[]{:S(2)}, u32[]{:S(2)}) collective-permute-start(f32[15,64,128]{2,1,0:T(8,128)S(1)} %bitcast.11), channel_id=1, source_target_pairs={{0,8},{1,9},{2,10},{3,11},{4,12},{5,13},{6,14},{7,15},{8,16},{9,17... | collective-permute-start | bytes 1474568 | tf_op jit(solution)/shard_map/ppermute | solution.py:384
  56.6 1.4 collective-permute-start.2
  58.1 2.4 %collective-permute-start.3 = (f32[15,64,128]{2,1,0:T(8,128)S(1)}, f32[15,64,128]{2,1,0:T(8,128)}, u32[]{:S(2)}, u32[]{:S(2)}) collective-permute-start(f32[15,64,128]{2,1,0:T(8,128)S(1)} %bitcast.13), channel_id=1, source_target_pairs={{0,4},{1,5},{2,6},{3,7},{4,0},{5,1},{6,2},{7,3},{8,12},{9,13},{10,... | collective-permute-start | bytes 1474568 | tf_op jit(solution)/shard_map/ppermute | solution.py:395
  60.5 0.1 collective-permute-start.4
  60.5 5.5 %copy.16.top_ref.e_ref = f32[126,64,64]{2,1,0:T(8,128)} copy(f32[126,64,64]{0,2,1:T(8,128)} %param.9) | data formatting | bytes 4128768 | tf_op args[2]
  66.1 0.0 copy-done
  66.1 0.0 copy-start.1
  66.1 1.6 copy-done.1
  67.7 8.2 %apply_local.1 = (f32[32,64,256]{2,1,0:T(8,128)}, f32[63,64,64]{2,1,0:T(8,128)}) custom-call(f32[64,64,128]{2,1,0:T(8,128)S(1)} %bitcast.8, f32[32,64,256]{2,1,0:T(8,128)} %v_ref.1, f32[63,64,64]{2,1,0:T(8,128)S(1)} %copy-done.1, f32[126,64,64]{2,1,0:T(8,128)} %copy.16.top_ref.e_ref), custom_call_target="tpu_custom_call" | custom-call | flops 9000000 | bytes 22500000 | tf_op jit(solution)/shard_map/apply_local/pallas_call | solution.py:236
  75.9 0.0 collective-permute-done.1
  75.9 0.0 collective-permute-done
  75.9 1.1 pad_maximum_fusion.refs_4_
  77.0 0.0 copy-start.4
  77.0 0.0 collective-permute-done.2.refs_1_
  77.0 4.6 %collective-permute-done.3.refs_2_ = f32[15,64,128]{2,1,0:T(8,128)} collective-permute-done((f32[15,64,128]{2,1,0:T(8,128)S(1)}, f32[15,64,128]{2,1,0:T(8,128)}, u32[]{:S(2)}, u32[]{:S(2)}) %collective-permute-start.3) | collective-permute-done | bytes 491552 | tf_op jit(solution)/shard_map/ppermute | solution.py:395
  81.7 0.0 collective-permute-done.4.refs_3_
  81.7 0.0 copy-done.3
  81.7 1.6 collective-permute-start.5
  83.3 0.1 collective-permute-start.6
  83.4 0.6 collective-permute-start.9
  84.0 2.4 %collective-permute-start.10 = (f32[30,64,128]{2,1,0:T(8,128)S(1)}, f32[30,64,128]{2,1,0:T(8,128)}, u32[]{:S(2)}, u32[]{:S(2)}) collective-permute-start(f32[30,64,128]{2,1,0:T(8,128)S(1)} %pad_maximum_fusion.refs_4_), channel_id=1, source_target_pairs={{0,4},{1,5},{2,6},{3,7},{4,0},{5,1},{6,2},{7,3},{8,12},{9,13},{10,... | collective-permute-start | bytes 2949128 | tf_op jit(solution)/shard_map/ppermute | solution.py:395
  86.4 0.3 collective-permute-start.11
  86.7 0.0 collective-permute-done.5.refs_8_
  86.7 0.8 copy-done.7
  87.5 1.3 collective-permute-start.7
  88.8 0.0 collective-permute-done.6.refs_9_
  88.8 0.0 collective-permute-start.8
  88.8 1.4 slice_bitcast_fusion.p_ref
  90.2 30.8 %top_tree.1 = (f32[126,64,64]{2,1,0:T(8,128)}, f32[64,64]{1,0:T(8,128)}, f32[64,64]{1,0:T(8,128)}) custom-call(s32[1]{0:T(128)} %bitcast.3.own_ref, f32[64,32,128]{2,1,0:T(8,128)} %all-gather.3.cloned.1.call-done.c_ref, f32[126,64,64]{2,1,0:T(8,128)} %copy.16.top_ref.e_ref, f32[64,64]{1,0:T(8,128)} %slice_bitcast_fusion.p_ref), custom_call_target="tpu_custom_call" | custom-call | flops 42000000 | bytes 105000000 | tf_op jit(solution)/shard_map/top_tree/pallas_call | solution.py:292
  121.0 0.0 collective-permute-done.7.refs_10_
  121.0 0.0 collective-permute-done.8.refs_11_
  121.0 0.0 collective-permute-done.9.refs_5_
  121.0 0.0 copy-start.5
  121.0 7.9 %collective-permute-done.10.refs_6_ = f32[30,64,128]{2,1,0:T(8,128)} collective-permute-done((f32[30,64,128]{2,1,0:T(8,128)S(1)}, f32[30,64,128]{2,1,0:T(8,128)}, u32[]{:S(2)}, u32[]{:S(2)}) %collective-permute-start.10) | collective-permute-done | bytes 983072 | tf_op jit(solution)/shard_map/ppermute | solution.py:395
  128.9 0.0 collective-permute-done.11.refs_7_
  129.0 0.0 copy-done.4
  129.0 1.6 collective-permute-start.12
  130.5 0.0 collective-permute-start.13
  130.5 0.5 collective-permute-start.14
  131.1 0.0 collective-permute-start.15
  131.1 0.0 copy-done.9
  131.1 0.1 copy.18
  131.1 0.7 fusion.8.where_ref
  131.9 4.8 %copy.21 = f32[126,64,64]{0,2,1:T(8,128)} copy(f32[126,64,64]{2,1,0:T(8,128)} %get-tuple-element.78) | data formatting | bytes 4128768
  136.7 0.0 copy-done.5
  136.7 0.0 copy-done.8
  136.7 0.6 bitcast_dynamic-update-slice_fusion
  137.3 0.0 collective-permute-done.12.refs_12_
  137.3 0.0 collective-permute-done.13.refs_13_
  137.3 1.0 copy-done.6
  138.3 0.0 collective-permute-done.14.refs_14_
  138.3 0.0 collective-permute-done.15.refs_15_
  138.3 29.0 %couple.1 = f32[56,8,64,64]{3,2,1,0:T(8,128)} custom-call(s32[56,8]{1,0:T(8,128)} %fusion.8.where_ref, f32[56,8,64,64]{3,2,1,0:T(8,128)} %s_ref.1, f32[64,64,128]{2,1,0:T(8,128)} %bitcast.9, f32[15,64,128]{2,1,0:T(8,128)} %bitcast.16, f32[15,64,128]{2,1,0:T(8,128)} %collective-permute-done.2.refs_1_, f32[15,64,128]{2,1,0:T(8,128)} %collective-permute-done.3.refs_2_, ...), custom_call_target="tpu_custom_call" | custom-call | flops 32000000 | bytes 80000000 | tf_op jit(solution)/shard_map/couple/pallas_call | solution.py:361
  (5 shorter events, 0.0 us)
Async XLA Ops:
  7.2 83.0 %all-gather.3.cloned.1.call-start = ((), (), s32[]{:S(2)}) async-start(), calls=%async_computation | async-start | bytes 1114112 | tf_op jit(solution)/shard_map/all_gather | solution.py:421
  31.4 1.6 copy-start.2
  49.2 16.9 %copy-start = (f32[4096,128]{1,0:T(8,128)}, f32[4096,128]{1,0:T(8,128)S(1)}, u32[]{:S(2)}) copy-start(f32[4096,128]{1,0:T(8,128)S(1)} %get-tuple-element.47) | copy-start | bytes 6291460
  49.2 32.4 %copy-start.3 = (f32[960,128]{1,0:T(8,128)}, f32[960,128]{1,0:T(8,128)S(1)}, u32[]{:S(2)}) copy-start(f32[960,128]{1,0:T(8,128)S(1)} %get-tuple-element.49) | copy-start | bytes 1474564
  49.2 26.6 %collective-permute-start.1 = (f32[15,64,128]{2,1,0:T(8,128)S(1)}, f32[15,64,128]{2,1,0:T(8,128)S(1)}, u32[]{:S(2)}, u32[]{:S(2)}) collective-permute-start(f32[15,64,128]{2,1,0:T(8,128)S(1)} %bitcast.10), channel_id=1, source_target_pairs={{8,0},{9,1},{10,2},{11,3},{12,4},{13,5},{14,6},{15,7},{16,8},{17,9... | collective-permute-start | bytes 1474568 | tf_op jit(solution)/shard_map/ppermute | solution.py:384
  51.7 24.2 %collective-permute-start = (f32[15,64,128]{2,1,0:T(8,128)S(1)}, f32[15,64,128]{2,1,0:T(8,128)}, u32[]{:S(2)}, u32[]{:S(2)}) collective-permute-start(f32[15,64,128]{2,1,0:T(8,128)S(1)} %bitcast.11), channel_id=1, source_target_pairs={{0,8},{1,9},{2,10},{3,11},{4,12},{5,13},{6,14},{7,15},{8,16},{9,17... | collective-permute-start | bytes 1474568 | tf_op jit(solution)/shard_map/ppermute | solution.py:384
  56.6 20.4 %collective-permute-start.2 = (f32[15,64,128]{2,1,0:T(8,128)S(1)}, f32[15,64,128]{2,1,0:T(8,128)}, u32[]{:S(2)}, u32[]{:S(2)}) collective-permute-start(f32[15,64,128]{2,1,0:T(8,128)S(1)} %bitcast.12), channel_id=1, source_target_pairs={{0,2},{1,3},{2,4},{3,5},{4,6},{5,7},{6,0},{7,1},{8,10},{9,11},{10,... | collective-permute-start | bytes 1474568 | tf_op jit(solution)/shard_map/ppermute | solution.py:395
  58.1 23.6 %collective-permute-start.3 = (f32[15,64,128]{2,1,0:T(8,128)S(1)}, f32[15,64,128]{2,1,0:T(8,128)}, u32[]{:S(2)}, u32[]{:S(2)}) collective-permute-start(f32[15,64,128]{2,1,0:T(8,128)S(1)} %bitcast.13), channel_id=1, source_target_pairs={{0,4},{1,5},{2,6},{3,7},{4,0},{5,1},{6,2},{7,3},{8,12},{9,13},{10,... | collective-permute-start | bytes 1474568 | tf_op jit(solution)/shard_map/ppermute | solution.py:395
  60.5 21.2 %collective-permute-start.4 = (f32[15,64,128]{2,1,0:T(8,128)S(1)}, f32[15,64,128]{2,1,0:T(8,128)}, u32[]{:S(2)}, u32[]{:S(2)}) collective-permute-start(f32[15,64,128]{2,1,0:T(8,128)S(1)} %bitcast.14), channel_id=1, source_target_pairs={{0,6},{1,7},{2,0},{3,1},{4,2},{5,3},{6,4},{7,5},{8,14},{9,15},{10,... | collective-permute-start | bytes 1474568 | tf_op jit(solution)/shard_map/ppermute | solution.py:395
  66.1 1.6 copy-start.1
  77.0 52.0 %copy-start.4 = (f32[30,64,128]{2,1,0:T(8,128)}, f32[30,64,128]{2,1,0:T(8,128)S(1)}, u32[]{:S(2)}) copy-start(f32[30,64,128]{2,1,0:T(8,128)S(1)} %pad_maximum_fusion.refs_4_) | copy-start | bytes 2949124
  81.7 5.0 %collective-permute-start.5 = (f32[15,64,128]{2,1,0:T(8,128)S(1)}, f32[15,64,128]{2,1,0:T(8,128)S(1)}, u32[]{:S(2)}, u32[]{:S(2)}) collective-permute-start(f32[15,64,128]{2,1,0:T(8,128)S(1)} %bitcast.15), channel_id=1, source_target_pairs={{0,1},{1,0},{2,3},{3,2},{4,5},{5,4},{6,7},{7,6},{8,9},{9,8},{10,11... | collective-permute-start | bytes 1474568 | tf_op jit(solution)/shard_map/ppermute | solution.py:389
  83.3 5.5 %collective-permute-start.6 = (f32[15,64,128]{2,1,0:T(8,128)}, f32[15,64,128]{2,1,0:T(8,128)}, u32[]{:S(2)}, u32[]{:S(2)}) collective-permute-start(f32[15,64,128]{2,1,0:T(8,128)} %collective-permute-done.2.refs_1_), channel_id=1, source_target_pairs={{0,1},{1,0},{2,3},{3,2},{4,5},{5,4},{6,7},{7,6},{8,9},{9,8},{10,11... | collective-permute-start | bytes 1474568 | tf_op jit(solution)/shard_map/ppermute | solution.py:389
  83.4 37.6 %collective-permute-start.9 = (f32[30,64,128]{2,1,0:T(8,128)S(1)}, f32[30,64,128]{2,1,0:T(8,128)S(1)}, u32[]{:S(2)}, u32[]{:S(2)}) collective-permute-start(f32[30,64,128]{2,1,0:T(8,128)S(1)} %pad_maximum_fusion.refs_4_), channel_id=1, source_target_pairs={{0,2},{1,3},{2,4},{3,5},{4,6},{5,7},{6,0},{7,1},{8,10},{9,11},{10,... | collective-permute-start | bytes 2949128 | tf_op jit(solution)/shard_map/ppermute | solution.py:395
  84.0 45.0 %collective-permute-start.10 = (f32[30,64,128]{2,1,0:T(8,128)S(1)}, f32[30,64,128]{2,1,0:T(8,128)}, u32[]{:S(2)}, u32[]{:S(2)}) collective-permute-start(f32[30,64,128]{2,1,0:T(8,128)S(1)} %pad_maximum_fusion.refs_4_), channel_id=1, source_target_pairs={{0,4},{1,5},{2,6},{3,7},{4,0},{5,1},{6,2},{7,3},{8,12},{9,13},{10,... | collective-permute-start | bytes 2949128 | tf_op jit(solution)/shard_map/ppermute | solution.py:395
  86.4 42.6 %collective-permute-start.11 = (f32[30,64,128]{2,1,0:T(8,128)S(1)}, f32[30,64,128]{2,1,0:T(8,128)}, u32[]{:S(2)}, u32[]{:S(2)}) collective-permute-start(f32[30,64,128]{2,1,0:T(8,128)S(1)} %pad_maximum_fusion.refs_4_), channel_id=1, source_target_pairs={{0,6},{1,7},{2,0},{3,1},{4,2},{5,3},{6,4},{7,5},{8,14},{9,15},{10,... | collective-permute-start | bytes 2949128 | tf_op jit(solution)/shard_map/ppermute | solution.py:395
  86.7 0.8 copy-start.7
  87.5 33.5 %collective-permute-start.7 = (f32[15,64,128]{2,1,0:T(8,128)}, f32[15,64,128]{2,1,0:T(8,128)}, u32[]{:S(2)}, u32[]{:S(2)}) collective-permute-start(f32[15,64,128]{2,1,0:T(8,128)} %collective-permute-done.3.refs_2_), channel_id=1, source_target_pairs={{0,1},{1,0},{2,3},{3,2},{4,5},{5,4},{6,7},{7,6},{8,9},{9,8},{10,11... | collective-permute-start | bytes 1474568 | tf_op jit(solution)/shard_map/ppermute | solution.py:389
  88.8 32.2 %collective-permute-start.8 = (f32[15,64,128]{2,1,0:T(8,128)}, f32[15,64,128]{2,1,0:T(8,128)}, u32[]{:S(2)}, u32[]{:S(2)}) collective-permute-start(f32[15,64,128]{2,1,0:T(8,128)} %collective-permute-done.4.refs_3_), channel_id=1, source_target_pairs={{0,1},{1,0},{2,3},{3,2},{4,5},{5,4},{6,7},{7,6},{8,9},{9,8},{10,11... | collective-permute-start | bytes 1474568 | tf_op jit(solution)/shard_map/ppermute | solution.py:389
  90.2 40.9 %copy-start.9 = (s32[56,8]{0,1:T(8,128)S(1)}, s32[56,8]{0,1:T(8,128)}, u32[]{:S(2)}) copy-start(s32[56,8]{0,1:T(8,128)} %param.11) | copy-start | bytes 5380
  121.0 15.7 %copy-start.5 = (f32[30,64,128]{2,1,0:T(8,128)}, f32[30,64,128]{2,1,0:T(8,128)S(1)}, u32[]{:S(2)}) copy-start(f32[30,64,128]{2,1,0:T(8,128)S(1)} %collective-permute-done.9.refs_5_) | copy-start | bytes 2949124
  129.0 8.4 %collective-permute-start.12 = (f32[30,64,128]{2,1,0:T(8,128)S(1)}, f32[30,64,128]{2,1,0:T(8,128)S(1)}, u32[]{:S(2)}, u32[]{:S(2)}) collective-permute-start(f32[30,64,128]{2,1,0:T(8,128)S(1)} %pad_maximum_fusion.refs_4_), channel_id=1, source_target_pairs={{0,1},{1,0},{2,3},{3,2},{4,5},{5,4},{6,7},{7,6},{8,9},{9,8},{10,11... | collective-permute-start | bytes 2949128 | tf_op jit(solution)/shard_map/ppermute | solution.py:389
  130.5 6.8 %collective-permute-start.13 = (f32[30,64,128]{2,1,0:T(8,128)S(1)}, f32[30,64,128]{2,1,0:T(8,128)}, u32[]{:S(2)}, u32[]{:S(2)}) collective-permute-start(f32[30,64,128]{2,1,0:T(8,128)S(1)} %collective-permute-done.9.refs_5_), channel_id=1, source_target_pairs={{0,1},{1,0},{2,3},{3,2},{4,5},{5,4},{6,7},{7,6},{8,9},{9,8},{10,11... | collective-permute-start | bytes 2949128 | tf_op jit(solution)/shard_map/ppermute | solution.py:389
  130.5 7.8 %collective-permute-start.14 = (f32[30,64,128]{2,1,0:T(8,128)}, f32[30,64,128]{2,1,0:T(8,128)}, u32[]{:S(2)}, u32[]{:S(2)}) collective-permute-start(f32[30,64,128]{2,1,0:T(8,128)} %collective-permute-done.10.refs_6_), channel_id=1, source_target_pairs={{0,1},{1,0},{2,3},{3,2},{4,5},{5,4},{6,7},{7,6},{8,9},{9,8},{10,11... | collective-permute-start | bytes 2949128 | tf_op jit(solution)/shard_map/ppermute | solution.py:389
  131.1 7.2 %collective-permute-start.15 = (f32[30,64,128]{2,1,0:T(8,128)}, f32[30,64,128]{2,1,0:T(8,128)}, u32[]{:S(2)}, u32[]{:S(2)}) collective-permute-start(f32[30,64,128]{2,1,0:T(8,128)} %collective-permute-done.11.refs_7_), channel_id=1, source_target_pairs={{0,1},{1,0},{2,3},{3,2},{4,5},{5,4},{6,7},{7,6},{8,9},{9,8},{10,11... | collective-permute-start | bytes 2949128 | tf_op jit(solution)/shard_map/ppermute | solution.py:389
  131.9 4.8 %copy-start.8 = (f32[64,64]{1,0:T(8,128)S(1)}, f32[64,64]{1,0:T(8,128)}, u32[]{:S(2)}) copy-start(f32[64,64]{1,0:T(8,128)} %get-tuple-element.59) | copy-start | bytes 49156
  137.3 1.0 copy-start.6
Sparse Core Ops, SparseCore 0:
  31.5 43.7 all-gather.2
